TPU v7x, 32 devices: a whole 2x2x4 slice. The times are simulated.
32 devices in a mesh: row: 4 (over y, core), col: 4 (over z), depth: 2 (over x).
Axes of the slice: x: 2, y: 2, z: 4, core: 2. Of those that a mesh axis runs over, the one named last changes fastest.
Arguments:
- gate_pre: bfloat16 [256, 26624], P(('col', 'depth'), 'row'), may hold values from -6 to 6
- up_pre: bfloat16 [256, 26624], P(('col', 'depth'), 'row'), may hold values from -6 to 6
- out_grad: bfloat16 [256, 16384], P(('row', 'depth'), 'col'), may hold values from -4 to 4
- down_weight: bfloat16 [26624, 16384], P('row', 'col'), may hold values from -0.0390625 to 0.0390625
Outputs:
- weight_grad: bfloat16 [26624, 16384], P(('row', 'depth'), 'col')
- gate_grad: bfloat16 [256, 26624], P(('col', 'depth'), 'row')
- up_grad: bfloat16 [256, 26624], P(('col', 'depth'), 'row')
All inputs are finite; a program needn't handle non-finite values.
Results may differ from a plain program's by a relative error of at most 0.009.
Values may be sent and summed in bfloat16 or wider, within the bound.
No kernel may reach another device: no remote copies, remote signals or barrier semaphores. Data moves between devices by JAX's collectives and lax.ppermute only.
A program may use at most 192 MiB of HBM per device.

v0:
```python
import jax
import jax.numpy as jnp
from jax import lax
from jax.sharding import PartitionSpec as P


def on_device(gate_pre, up_pre, out_grad, down_weight):
    gate_vals = gate_pre.astype(jnp.float32)
    up_vals = up_pre.astype(jnp.float32)
    sigma_gate = jax.nn.sigmoid(gate_vals)
    act = gate_vals * sigma_gate
    gate_all, up_all = (
        lax.all_gather(gate_pre, "col", axis=0, tiled=True),
        lax.all_gather(up_pre, "col", axis=0, tiled=True),
    )
    gate_wide = gate_all.astype(jnp.float32)
    hidden_all = (gate_wide * jax.nn.sigmoid(gate_wide) * up_all.astype(jnp.float32)).astype(
        jnp.bfloat16
    )
    grads_all = lax.all_gather(out_grad, "row", axis=0, tiled=True)
    weight_terms = lax.dot_general(
        hidden_all, grads_all, (((0,), (0,)), ((), ())), preferred_element_type=jnp.float32
    )
    hidden_terms = lax.dot_general(
        grads_all, down_weight, (((1,), (1,)), ((), ())), preferred_element_type=jnp.float32
    )
    hidden_grad = lax.psum_scatter(hidden_terms, "col", scatter_dimension=0, tiled=True)
    up_grad = (hidden_grad * act).astype(jnp.bfloat16)
    gate_grad = (
        hidden_grad * up_vals * sigma_gate * (1.0 + gate_vals * (1.0 - sigma_gate))
    ).astype(jnp.bfloat16)
    layer_partial = weight_terms.astype(jnp.bfloat16)
    weight_grad = (
        lax.psum_scatter(layer_partial, "depth", scatter_dimension=0, tiled=True)
        .astype(jnp.float32)
        .astype(jnp.bfloat16)
    )
    return (weight_grad, gate_grad, up_grad)


def solution(mesh):
    placed = (
        P(("col", "depth"), "row"),
        P(("col", "depth"), "row"),
        P(("row", "depth"), "col"),
        P("row", "col"),
    )
    return jax.shard_map(
        on_device,
        mesh=mesh,
        in_specs=placed,
        out_specs=(
            P(("row", "depth"), "col"),
            P(("col", "depth"), "row"),
            P(("col", "depth"), "row"),
        ),
        check_vma=False,
    )
```

profile of v0, /device:TPU:0, one launch (start us, length us, event | category | flops | bytes accessed | tf_op | source)
XLA Modules:
  0.0 778.4 jit_solution(7507167107155119052)
XLA Ops:
  7.2 0.0 all-gather.8.cloned.1.call-start
  7.2 0.7 all-gather.8.cloned.1.call-update
  7.9 0.0 all-gather.4.cloned.1.call-start
  7.9 0.7 all-gather.4.cloned.1.call-update
  8.6 0.0 all-gather.6.cloned.1.call-start
  8.7 0.7 all-gather.6.cloned.1.call-update
  9.4 0.0 reduce-scatter.5.cloned.1.call-start
  9.4 19.6 %all-gather.8.cloned.1.call-done = bf16[128,4096]{1,0:T(8,128)(2,1)} async-done(((bf16[32,4096]{1,0:T(8,128)(2,1)}), bf16[128,4096]{1,0:T(8,128)(2,1)}) %all-gather.8.cloned.1.call-update) | async-done | bytes 1048592 | tf_op jit(solution)/shard_map/all_gather | solution.py:20
  29.0 25.0 %fusion.16 = f32[128,6656]{1,0:T(8,128)} fusion(bf16[128,4096]{1,0:T(8,128)(2,1)} %all-gather.8.cloned.1.call-done, bf16[6656,4096]{1,0:T(8,128)(2,1)} %param.7), kind=kOutput, calls=%fused_computation.21 | convolution fusion | flops 6979321856 | bytes 58982400 | tf_op jit(solution)/shard_map/dot_general | solution.py:24
  54.0 0.0 copy-start
  54.0 0.0 reduce-scatter.5.cloned.1.call-update
  54.1 0.0 reduce-scatter.7.cloned.1.call-start
  54.1 15.8 %all-gather.4.cloned.1.call-done = bf16[128,6656]{1,0:T(8,128)(2,1)} async-done(((bf16[32,6656]{1,0:T(8,128)(2,1)}), bf16[128,6656]{1,0:T(8,128)(2,1)}) %all-gather.4.cloned.1.call-update) | async-done | bytes 1703952 | tf_op jit(solution)/shard_map/all_gather | solution.py:13
  69.9 39.7 %all-gather.6.cloned.1.call-done = bf16[128,6656]{1,0:T(8,128)(2,1)} async-done(((bf16[32,6656]{1,0:T(8,128)(2,1)}), bf16[128,6656]{1,0:T(8,128)(2,1)}) %all-gather.6.cloned.1.call-update) | async-done | bytes 1703952 | tf_op jit(solution)/shard_map/all_gather | solution.py:14
  109.6 0.0 copy-done
  109.6 23.9 %convolution_convert_fusion = bf16[6656,4096]{1,0:T(8,128)(2,1)} fusion(bf16[128,4096]{1,0:T(8,128)(2,1)S(1)} %copy-done, bf16[128,6656]{1,0:T(8,128)(2,1)} %all-gather.6.cloned.1.call-done, bf16[128,6656]{1,0:T(8,128)(2,1)} %all-gather.4.cloned.1.call-done), kind=kOutput, calls=%fused_computation | convolution fusion | flops 7013400576 | bytes 58982400 | tf_op jit(solution)/shard_map/dot_general | solution.py:21
  133.4 0.0 copy-start.1
  133.4 0.0 copy-start.2
  133.4 0.0 reduce-scatter.7.cloned.1.call-update
  133.5 41.5 %reduce-scatter.5.cloned.1.call-done = f32[32,6656]{1,0:T(8,128)} async-done(((f32[128,6656]{1,0:T(8,128)}), f32[32,6656]{1,0:T(8,128)}) %reduce-scatter.5.cloned.1.call-update) | async-done | bytes 851984 | tf_op jit(solution)/shard_map/reduce_scatter | solution.py:27
  174.9 0.0 copy-done.1
  174.9 0.0 copy-done.2
  174.9 2.5 fusion.14
  177.4 594.4 %reduce-scatter.7.cloned.1.call-done = bf16[3328,4096]{1,0:T(8,128)(2,1)} async-done(((bf16[6656,4096]{1,0:T(8,128)(2,1)}), bf16[3328,4096]{1,0:T(8,128)(2,1)}) %reduce-scatter.7.cloned.1.call-update) | async-done | bytes 27262992
Async XLA Ops:
  7.2 21.9 %all-gather.8.cloned.1.call-start = ((), (), s32[]{:S(2)}) async-start(), calls=%async_computation.4 | async-start | bytes 1310720 | tf_op jit(solution)/shard_map/all_gather | solution.py:20
  7.9 62.0 %all-gather.4.cloned.1.call-start = ((), (), s32[]{:S(2)}) async-start(), calls=%async_computation.2 | async-start | bytes 2129920 | tf_op jit(solution)/shard_map/all_gather | solution.py:13
  8.6 100.9 %all-gather.6.cloned.1.call-start = ((), (), s32[]{:S(2)}) async-start(), calls=%async_computation.3 | async-start | bytes 2129920 | tf_op jit(solution)/shard_map/all_gather | solution.py:14
  9.4 165.6 %reduce-scatter.5.cloned.1.call-start = ((), (), s32[]{:S(2)}) async-start(), calls=%async_computation.5 | async-start | bytes 4259840 | tf_op jit(solution)/shard_map/reduce_scatter | solution.py:27
  54.0 55.5 %copy-start = (bf16[128,4096]{1,0:T(8,128)(2,1)S(1)}, bf16[128,4096]{1,0:T(8,128)(2,1)}, u32[]{:S(2)}) copy-start(bf16[128,4096]{1,0:T(8,128)(2,1)} %all-gather.8.cloned.1.call-done) | copy-start | bytes 3145732
  54.1 717.8 %reduce-scatter.7.cloned.1.call-start = ((), (), s32[]{:S(2)}) async-start(), calls=%async_computation.6 | async-start | bytes 81788928
  133.4 41.5 %copy-start.1 = (bf16[32,6656]{1,0:T(8,128)(2,1)S(1)}, bf16[32,6656]{1,0:T(8,128)(2,1)}, u32[]{:S(2)}) copy-start(bf16[32,6656]{1,0:T(8,128)(2,1)} %param.4) | copy-start | bytes 1277956
  133.4 41.5 %copy-start.2 = (bf16[32,6656]{1,0:T(8,128)(2,1)S(1)}, bf16[32,6656]{1,0:T(8,128)(2,1)}, u32[]{:S(2)}) copy-start(bf16[32,6656]{1,0:T(8,128)(2,1)} %param.5) | copy-start | bytes 1277956
Sparse Core Ops, SparseCore 0:
  9.6 19.4 all-gather.7
  30.6 39.2 all-gather.3
  71.5 38.0 all-gather.5
  111.7 63.1 reduce-scatter.4
  177.7 594.1 reduce-scatter.6
where the time goes:
time: 779 us; the launch traced here: 778 us
  waiting for transfers between devices  713 us (92%)
  matrix products  48.9 us (6%)
  between operations  13.8 us (2%)
    unnamed x6, waiting for transfers between devices  597 us
    reduce_scatter x1, waiting for transfers between devices, on_device(): lax.psum_scatter(hidden_terms, 'col', scatter_dimension=0, tiled=True)  41.5 us
    all_gather x1, waiting for transfers between devices, on_device(): lax.all_gather(up_pre, 'col', axis=0, tiled=True)  39.7 us
    dot_general x1, matrix products, on_device(): lax.dot_general(grads_all, down_weight, (((1,), (1,)), ((), ())), preferr...  25 us
    dot_general x1, matrix products, on_device(): lax.dot_general(hidden_all, grads_all, (((0,), (0,)), ((), ())), preferre...  23.9 us
    all_gather x1, waiting for transfers between devices, on_device(): grads_all = lax.all_gather(out_grad, 'row', axis=0, tiled=True)  19.6 us
    all_gather x1, waiting for transfers between devices, on_device(): lax.all_gather(gate_pre, 'col', axis=0, tiled=True)  15.8 us
  transfers between devices with their start and end apart: 5, of which 5 were waited for; matrix products, arithmetic and copies ran while one was open for 7% of the time, Pallas kernels for 0%

commit v1 on v0

v1 whole, which is shorter than its diff:
```python
import functools

import jax
import jax.numpy as jnp
from jax import lax
from jax.experimental import pallas as pl
from jax.experimental.pallas import tpu as pltpu
from jax.sharding import PartitionSpec as P

BF16 = jnp.bfloat16
QUICK = pl.CostEstimate(flops=1, bytes_accessed=1, transcendentals=0)
F32 = jnp.float32


def xor_pairs(size, distance):
    return [(i, i ^ distance) for i in range(size)]


def block_copies(shift, refs, scratch, base, tok, sems):
    copies = []
    for i, (value, ref) in enumerate(zip((0, 2, 1, 3), refs)):
        start = pl.multiple_of(base + jnp.bitwise_xor(shift, value) * tok, tok)
        copies.append(
            pltpu.make_async_copy(ref, scratch.at[pl.ds(start, tok)], sems.at[i])
        )
    return copies


def hidden_kernel(depth_ref, gate_ref, up_ref, mine, theirs):
    half = mine.shape[1]
    for ref, at in ((mine, depth_ref[0]), (theirs, 1 - depth_ref[0])):
        columns = pl.ds(pl.multiple_of(at * half, 128), half)
        gate = gate_ref[:, columns].astype(F32)
        up = up_ref[:, columns].astype(F32)
        ref[...] = (gate * jax.nn.sigmoid(gate) * up).astype(ref.dtype)


def hidden_halves(depth, gate_pre, up_pre):
    tok, ff = gate_pre.shape
    vmem = pl.BlockSpec(memory_space=pltpu.VMEM)
    return pl.pallas_call(
        hidden_kernel,
        out_shape=[jax.ShapeDtypeStruct((tok, ff // 2), BF16)] * 2,
        in_specs=[pl.BlockSpec(memory_space=pltpu.SMEM), vmem, vmem],
        out_specs=[vmem, vmem],
        compiler_params=pltpu.CompilerParams(vmem_limit_bytes=8 << 20),
        cost_estimate=QUICK,
    )(depth, gate_pre, up_pre)


def cuts(rows, most):
    parts = -(-rows // most)
    step = -(-rows // parts // 128) * 128
    return [(at, min(step, rows - at)) for at in range(0, rows, step)]


def in_hbm(arrays):
    return [pltpu.with_memory_space_constraint(x, pltpu.HBM) for x in arrays]


ANYWHERE = pl.BlockSpec(memory_space=pl.ANY)
VMEM = pl.BlockSpec(memory_space=pltpu.VMEM)
SMEM = pl.BlockSpec(memory_space=pltpu.SMEM)


def partial_kernel(tok, first, tiles, n_after, shift_ref, *refs):
    grads_in, w_ref, refs = refs[:4], refs[4], refs[5 + n_after :]
    terms_out, (grads, rows, sems, w_sems) = refs[:4], refs[4:]
    copies = block_copies(shift_ref[0], grads_in, grads, 0, tok, sems)
    fetches = [
        pltpu.make_async_copy(
            w_ref.at[pl.ds(first + at, size)], rows.at[pl.ds(at, size)], w_sems.at[i]
        )
        for i, (at, size) in enumerate(tiles)
    ]
    for copy in copies:
        copy.start()
    for copy in copies:
        copy.wait()
    for fetch in fetches:
        fetch.start()
    for fetch, (at, size) in zip(fetches, tiles):
        fetch.wait()
        terms = lax.dot_general(
            grads[...],
            rows[at : at + size, :],
            (((1,), (1,)), ((), ())),
            preferred_element_type=F32,
        )
        for k, ref in enumerate(terms_out):
            ref[:, at : at + size] = terms[k * tok : (k + 1) * tok].astype(ref.dtype)


def partials(shift, grads, weight, first, rows, after):
    tok, width = grads[0].shape
    tiles = [(0, 256)] + [(256 + at, size) for at, size in cuts(rows - 256, 512)]
    return pl.pallas_call(
        functools.partial(partial_kernel, tok, first, tiles, len(after)),
        out_shape=[jax.ShapeDtypeStruct((tok, rows), F32)]
        + [jax.ShapeDtypeStruct((tok, rows), BF16)] * 3,
        in_specs=[SMEM] + [ANYWHERE] * (5 + len(after)),
        out_specs=[VMEM] * 4,
        scratch_shapes=[
            pltpu.VMEM((4 * tok, width), BF16),
            pltpu.VMEM((rows, width), BF16),
            pltpu.SemaphoreType.DMA((4,)),
            pltpu.SemaphoreType.DMA((len(tiles),)),
        ],
        compiler_params=pltpu.CompilerParams(vmem_limit_bytes=40 << 20),
        cost_estimate=QUICK,
    )(shift, *in_hbm([*grads, weight, *after]))


def outer_kernel(tok, tile, shift_ref, *refs):
    out_ref, token, grads, hidden, ready, sems, in_sems = refs[16:]
    token[...] = jnp.zeros_like(token)
    copies = []
    for half in range(2):
        base = 4 * tok * half
        copies += block_copies(
            shift_ref[0], refs[4 * half : 4 * half + 4], grads, base, tok, in_sems.at[half]
        )
        for k, ref in zip((0, 2, 1, 3), refs[8 + 4 * half : 12 + 4 * half]):
            rows = pl.ds(base + k * tok, tok)
            copies.append(
                pltpu.make_async_copy(ref, hidden.at[rows], in_sems.at[half, 4 + k])
            )
    for copy in copies:
        copy.start()
    for copy in copies:
        copy.wait()
    steps = hidden.shape[1] // tile
    slots = ready.shape[0]

    def copy_out(i):
        return pltpu.make_async_copy(
            ready.at[i % slots], out_ref.at[pl.ds(i * tile, tile)], sems.at[i % slots]
        )

    for i in range(steps):
        if i >= slots:
            copy_out(i - slots).wait()
        ready[i % slots] = lax.dot_general(
            hidden[:, i * tile : (i + 1) * tile],
            grads[...],
            (((0,), (0,)), ((), ())),
            preferred_element_type=F32,
        ).astype(BF16)
        copy_out(i).start()
    for i in range(steps - slots, steps):
        copy_out(i).wait()


def outer(shift, grads, hidden, tile=128, slots=26):
    tok, width = grads[0].shape
    rows = hidden[0].shape[1]
    return pl.pallas_call(
        functools.partial(outer_kernel, tok, tile),
        out_shape=[
            jax.ShapeDtypeStruct((rows, width), BF16),
            jax.ShapeDtypeStruct((8, 128), F32),
        ],
        in_specs=[SMEM] + [ANYWHERE] * 16,
        out_specs=[ANYWHERE, VMEM],
        scratch_shapes=[
            pltpu.VMEM((8 * tok, width), BF16),
            pltpu.VMEM((8 * tok, rows), BF16),
            pltpu.VMEM((slots, tile, width), BF16),
            pltpu.SemaphoreType.DMA((slots,)),
            pltpu.SemaphoreType.DMA((2, 8)),
        ],
        compiler_params=pltpu.CompilerParams(vmem_limit_bytes=40 << 20),
        cost_estimate=QUICK,
    )(shift, *in_hbm(grads), *in_hbm(hidden))


def finish(hidden_grad, gate_vals, up_vals):
    sigma_gate = jax.nn.sigmoid(gate_vals)
    up_grad = (hidden_grad * (gate_vals * sigma_gate)).astype(BF16)
    gate_grad = (
        hidden_grad * up_vals * sigma_gate * (1.0 + gate_vals * (1.0 - sigma_gate))
    ).astype(BF16)
    return gate_grad, up_grad


def finish_kernel(parts, gate_ref, up_ref, *refs):
    gate_out, up_out = refs[-2:]
    at = 0
    for i in range(parts):
        p0, r1, r2, r3 = refs[4 * i : 4 * i + 4]
        columns = slice(at, at + p0.shape[1])
        total = p0[...] + r1[...].astype(F32) + r2[...].astype(F32) + r3[...].astype(F32)
        gate_out[:, columns], up_out[:, columns] = finish(
            total, gate_ref[:, columns].astype(F32), up_ref[:, columns].astype(F32)
        )
        at += p0.shape[1]


def finished(gate_pre, up_pre, sums, after):
    vmem = pl.BlockSpec(memory_space=pltpu.VMEM)
    terms = [term for part in sums for term in part]
    return pl.pallas_call(
        functools.partial(finish_kernel, len(sums)),
        out_shape=[jax.ShapeDtypeStruct(gate_pre.shape, BF16)] * 2,
        in_specs=[vmem] * (2 + len(terms)) + [pl.BlockSpec(memory_space=pl.ANY)],
        out_specs=[vmem, vmem],
        compiler_params=pltpu.CompilerParams(vmem_limit_bytes=16 << 20),
    )(gate_pre, up_pre, *terms, after)


def by_distance(gate_pre, up_pre, out_grad, down_weight):
    ff = gate_pre.shape[1]
    half = ff // 2
    row, col, depth = (lax.axis_index(a) for a in ("row", "col", "depth"))
    shift = jnp.bitwise_xor(row, col).astype(jnp.int32).reshape(1)

    def send(x, axis, distance):
        return lax.ppermute(x, axis, xor_pairs(lax.axis_size(axis), distance))

    g0 = out_grad
    g2 = send(g0, "row", 2)
    g1 = send(g0, "row", 1)
    g3 = send(g2, "row", 1)

    mine, theirs = hidden_halves(depth.astype(jnp.int32).reshape(1), gate_pre, up_pre)
    other = send(theirs, "depth", 1)

    def gather_col(x):
        x2 = send(x, "col", 2)
        return x, x2, send(x, "col", 1), send(x2, "col", 1)

    own_layer = gather_col(mine)
    other_layer = gather_col(other)

    q0 = send(g0, "depth", 1)
    q2 = send(q0, "row", 2)
    q1 = send(q0, "row", 1)
    q3 = send(q2, "row", 1)

    grads = (g0, g2, g1, g3)
    def reduced(terms):
        p0, p1, p2, p3 = terms
        r2, r3, r1 = send(p2, "col", 2), send(p3, "col", 3), send(p1, "col", 1)
        return p0, r1, r2, r3

    after = (own_layer[1], q0)
    sums = [reduced(partials(shift, grads, down_weight, 0, half, after))]
    after = (own_layer[2], other_layer[1], other_layer[2], q2)
    sums.append(reduced(partials(shift, grads, down_weight, half, ff - half, after)))
    weight_grad, token = outer(shift, grads + (q0, q2, q1, q3), own_layer + other_layer)
    gate_grad, up_grad = finished(gate_pre, up_pre, sums, token)
    return weight_grad, gate_grad, up_grad


def by_collectives(gate_pre, up_pre, out_grad, down_weight):
    tok, ff = gate_pre.shape
    n_row, n_depth = lax.axis_size("row"), lax.axis_size("depth")
    gate_vals = gate_pre.astype(F32)
    up_vals = up_pre.astype(F32)
    hidden = (gate_vals * jax.nn.sigmoid(gate_vals) * up_vals).astype(BF16)
    layers = lax.all_to_all(hidden, "depth", split_axis=1, concat_axis=0, tiled=True)
    hidden_all = lax.all_gather(layers, "col", axis=0, tiled=True)
    grads_all = lax.all_gather(out_grad, ("row", "depth"), axis=0, tiled=True)
    weight_grad = lax.dot_general(
        hidden_all, grads_all, (((0,), (0,)), ((), ())), preferred_element_type=F32
    ).astype(BF16)
    layer = lax.dynamic_index_in_dim(
        grads_all.reshape(n_row, n_depth, tok, -1), lax.axis_index("depth"), 1, False
    ).reshape(n_row * tok, -1)
    hidden_terms = lax.dot_general(
        layer, down_weight, (((1,), (1,)), ((), ())), preferred_element_type=F32
    )
    hidden_grad = lax.psum_scatter(hidden_terms, "col", scatter_dimension=0, tiled=True)
    gate_grad, up_grad = finish(hidden_grad, gate_vals, up_vals)
    return weight_grad, gate_grad, up_grad


def solution(mesh):
    sizes = tuple(mesh.shape[a] for a in ("row", "col", "depth"))
    placed = (
        P(("col", "depth"), "row"),
        P(("col", "depth"), "row"),
        P(("row", "depth"), "col"),
        P("row", "col"),
    )
    return jax.shard_map(
        by_distance if sizes == (4, 4, 2) else by_collectives,
        mesh=mesh,
        in_specs=placed,
        out_specs=(
            P(("row", "depth"), "col"),
            P(("col", "depth"), "row"),
            P(("col", "depth"), "row"),
        ),
        check_vma=False,
    )
```

time: 779 us -> 100 us (0.13)
  the two profiles are of different devices: /device:TPU:0 before, /device:TPU:18 now
where the time goes in v1:
time: 100 us; the launch traced here: 99.7 us
  Pallas kernels  40.2 us (40%)
  waiting for transfers between devices  32.8 us (33%)
  starting transfers between devices  23.2 us (23%)
  local copies, waits for them, and re-layouts  2.73 us (3%)
    ppermute x20, waiting for transfers between devices, send(): return lax.ppermute(x, axis, xor_pairs(lax.axis_size(axis), distance))  32.8 us
    pallas_call x2, Pallas kernels, partials(): pl.pallas_call(functools.partial(partial_kernel, tok, first, tiles, len(a...  26.7 us
    ppermute x20, starting transfers between devices, send(): return lax.ppermute(x, axis, xor_pairs(lax.axis_size(axis), distance))  23.2 us
    pallas_call x1, Pallas kernels, outer(): pl.pallas_call(functools.partial(outer_kernel, tok, tile), out_shape=[jax...  11.8 us
    unnamed x38, local copies, waits for them, and re-layouts  2.73 us
  transfers between devices with their start and end apart: 20, of which 7 were waited for; matrix products, arithmetic and copies ran while one was open for 0% of the time, Pallas kernels for 39%

profile of v1, /device:TPU:18, one launch (start us, length us, event | category | flops | bytes accessed | tf_op | source)
XLA Modules:
  0.0 99.7 jit_solution(7386130585480041933)
XLA Ops:
  0.6 0.6 collective-permute-start.3
  1.2 1.0 %copy-done = bf16[32,6656]{1,0:T(8,128)(2,1)S(1)} copy-done((bf16[32,6656]{1,0:T(8,128)(2,1)S(1)}, bf16[32,6656]{1,0:T(8,128)(2,1)}, u32[]{:S(2)}) %copy-start) | copy-done | bytes 426008
  2.2 1.0 %copy-done.2 = bf16[32,6656]{1,0:T(8,128)(2,1)S(1)} copy-done((bf16[32,6656]{1,0:T(8,128)(2,1)S(1)}, bf16[32,6656]{1,0:T(8,128)(2,1)}, u32[]{:S(2)}) %copy-start.2) | copy-done | bytes 426008
  3.2 0.2 shard_map.67
  3.4 1.6 %collective-permute-start.10 = (bf16[32,3328]{1,0:T(8,128)(2,1)S(1)}, bf16[32,3328]{1,0:T(8,128)(2,1)S(1)}, u32[]{:S(2)}, u32[]{:S(2)}) collective-permute-start(bf16[32,3328]{1,0:T(8,128)(2,1)S(1)} %get-tuple-element.18), channel_id=1, source_target_pairs={{0,1},{1,0},{2,3},{3,2},{4,5},{5,4},{6,7},{7,6},{8,9},{9,8},{10,11... | collective-permute-start | bytes 638984 | tf_op jit(solution)/shard_map/ppermute | solution.py:218
  5.0 1.5 %collective-permute-start = (bf16[32,4096]{1,0:T(8,128)(2,1)}, bf16[32,4096]{1,0:T(8,128)(2,1)S(1)}, u32[]{:S(2)}, u32[]{:S(2)}) collective-permute-start(bf16[32,4096]{1,0:T(8,128)(2,1)} %refs_0_.5), channel_id=1, source_target_pairs={{0,16},{8,24},{16,0},{24,8},{1,17},{9,25},{17,1},{25,9},{2,18},{10... | collective-permute-start | bytes 786440 | tf_op jit(solution)/shard_map/ppermute | solution.py:218
  6.5 0.3 collective-permute-start.7
  6.9 1.6 %collective-permute-start.8 = (bf16[32,3328]{1,0:T(8,128)(2,1)S(1)}, bf16[32,3328]{1,0:T(8,128)(2,1)S(1)}, u32[]{:S(2)}, u32[]{:S(2)}) collective-permute-start(bf16[32,3328]{1,0:T(8,128)(2,1)S(1)} %get-tuple-element.17.refs_8_), channel_id=1, source_target_pairs={{0,2},{2,0},{4,6},{6,4},{1,3},{3,1},{5,7},{7,5},{8,10},{10,8},{12,... | collective-permute-start | bytes 638984 | tf_op jit(solution)/shard_map/ppermute | solution.py:218
  8.4 5.1 %collective-permute-done.10.refs_12_ = bf16[32,3328]{1,0:T(8,128)(2,1)S(1)} collective-permute-done((bf16[32,3328]{1,0:T(8,128)(2,1)S(1)}, bf16[32,3328]{1,0:T(8,128)(2,1)S(1)}, u32[]{:S(2)}, u32[]{:S(2)}) %collective-permute-start.10) | collective-permute-done | bytes 213024 | tf_op jit(solution)/shard_map/ppermute | solution.py:218
  13.5 1.6 %collective-permute-start.4 = (bf16[32,4096]{1,0:T(8,128)(2,1)S(1)}, bf16[32,4096]{1,0:T(8,128)(2,1)S(1)}, u32[]{:S(2)}, u32[]{:S(2)}) collective-permute-start(bf16[32,4096]{1,0:T(8,128)(2,1)S(1)} %collective-permute-done.3.refs_4_.refs_6_), channel_id=1, source_target_pairs={{0,16},{8,24},{16,0},{24,8},{1,17},{9,25},{17,1},{25,9},{2,18},{10... | collective-permute-start | bytes 786440 | tf_op jit(solution)/shard_map/ppermute | solution.py:218
  15.1 0.2 collective-permute-start.2
  15.3 0.3 collective-permute-done.7.refs_9_.refs_5_
  15.6 3.0 %collective-permute-start.11 = (bf16[32,3328]{1,0:T(8,128)(2,1)S(1)}, bf16[32,3328]{1,0:T(8,128)(2,1)S(1)}, u32[]{:S(2)}, u32[]{:S(2)}) collective-permute-start(bf16[32,3328]{1,0:T(8,128)(2,1)S(1)} %collective-permute-done.10.refs_12_), channel_id=1, source_target_pairs={{0,4},{2,6},{4,0},{6,2},{1,5},{3,7},{5,1},{7,3},{8,12},{10,14},{12... | collective-permute-start | bytes 638984 | tf_op jit(solution)/shard_map/ppermute | solution.py:218
  18.6 1.1 %collective-permute-start.12 = (bf16[32,3328]{1,0:T(8,128)(2,1)S(1)}, bf16[32,3328]{1,0:T(8,128)(2,1)S(1)}, u32[]{:S(2)}, u32[]{:S(2)}) collective-permute-start(bf16[32,3328]{1,0:T(8,128)(2,1)S(1)} %collective-permute-done.10.refs_12_), channel_id=1, source_target_pairs={{0,2},{2,0},{4,6},{6,4},{1,3},{3,1},{5,7},{7,5},{8,10},{10,8},{12,... | collective-permute-start | bytes 638984 | tf_op jit(solution)/shard_map/ppermute | solution.py:218
  19.7 2.6 %collective-permute-done.4.refs_5_.refs_8_ = bf16[32,4096]{1,0:T(8,128)(2,1)S(1)} collective-permute-done((bf16[32,4096]{1,0:T(8,128)(2,1)S(1)}, bf16[32,4096]{1,0:T(8,128)(2,1)S(1)}, u32[]{:S(2)}, u32[]{:S(2)}) %collective-permute-start.4) | collective-permute-done | bytes 262176 | tf_op jit(solution)/shard_map/ppermute | solution.py:218
  22.3 4.4 %collective-permute-done.11.refs_13_.refs_6_ = bf16[32,3328]{1,0:T(8,128)(2,1)S(1)} collective-permute-done((bf16[32,3328]{1,0:T(8,128)(2,1)S(1)}, bf16[32,3328]{1,0:T(8,128)(2,1)S(1)}, u32[]{:S(2)}, u32[]{:S(2)}) %collective-permute-start.11) | collective-permute-done | bytes 213024 | tf_op jit(solution)/shard_map/ppermute | solution.py:218
  26.7 3.1 %collective-permute-start.9 = (bf16[32,3328]{1,0:T(8,128)(2,1)S(1)}, bf16[32,3328]{1,0:T(8,128)(2,1)S(1)}, u32[]{:S(2)}, u32[]{:S(2)}) collective-permute-start(bf16[32,3328]{1,0:T(8,128)(2,1)S(1)} %collective-permute-done.7.refs_9_.refs_5_), channel_id=1, source_target_pairs={{0,2},{2,0},{4,6},{6,4},{1,3},{3,1},{5,7},{7,5},{8,10},{10,8},{12,... | collective-permute-start | bytes 638984 | tf_op jit(solution)/shard_map/ppermute | solution.py:218
  29.8 1.6 %collective-permute-start.13 = (bf16[32,3328]{1,0:T(8,128)(2,1)S(1)}, bf16[32,3328]{1,0:T(8,128)(2,1)S(1)}, u32[]{:S(2)}, u32[]{:S(2)}) collective-permute-start(bf16[32,3328]{1,0:T(8,128)(2,1)S(1)} %collective-permute-done.11.refs_13_.refs_6_), channel_id=1, source_target_pairs={{0,2},{2,0},{4,6},{6,4},{1,3},{3,1},{5,7},{7,5},{8,10},{10,8},{12,... | collective-permute-start | bytes 638984 | tf_op jit(solution)/shard_map/ppermute | solution.py:218
  31.5 0.7 copy-done.7
  32.1 13.3 %shard_map.70 = (f32[32,3328]{1,0:T(8,128)S(1)}, bf16[32,3328]{1,0:T(8,128)(2,1)S(1)}, bf16[32,3328]{1,0:T(8,128)(2,1)S(1)}, bf16[32,3328]{1,0:T(8,128)(2,1)S(1)}) custom-call(s32[1]{0:T(128)} %bitcast.shift_ref, bf16[32,4096]{1,0:T(8,128)(2,1)} %refs_0_.5, bf16[32,4096]{1,0:T(8,128)(2,1)} %copy-done.5, bf16[32,4096]{1,0:T(8,128)(2,1)} %copy-done.6, ...), custom_call_target="tpu_custom_call" | custom-call | flops 1 | bytes 1 | tf_op jit(solution)/shard_map/pallas_call | solution.py:97
  45.5 0.5 collective-permute-start.17
  46.0 13.4 %shard_map.69 = (f32[32,3328]{1,0:T(8,128)S(1)}, bf16[32,3328]{1,0:T(8,128)(2,1)S(1)}, bf16[32,3328]{1,0:T(8,128)(2,1)S(1)}, bf16[32,3328]{1,0:T(8,128)(2,1)S(1)}) custom-call(s32[1]{0:T(128)} %bitcast.shift_ref, bf16[32,4096]{1,0:T(8,128)(2,1)} %refs_0_.5, bf16[32,4096]{1,0:T(8,128)(2,1)} %copy-done.5, bf16[32,4096]{1,0:T(8,128)(2,1)} %copy-done.6, ...), custom_call_target="tpu_custom_call" | custom-call | flops 1 | bytes 1 | tf_op jit(solution)/shard_map/pallas_call | solution.py:97
  59.4 0.4 collective-permute-start.18
  59.9 2.7 %collective-permute-start.19 = (bf16[32,3328]{1,0:T(8,128)(2,1)S(1)}, bf16[32,3328]{1,0:T(8,128)(2,1)S(1)}, u32[]{:S(2)}, u32[]{:S(2)}) collective-permute-start(bf16[32,3328]{1,0:T(8,128)(2,1)S(1)} %get-tuple-element.27), channel_id=1, source_target_pairs={{0,6},{2,4},{4,2},{6,0},{1,7},{3,5},{5,3},{7,1},{8,14},{10,12},{12... | collective-permute-start | bytes 638984 | tf_op jit(solution)/shard_map/ppermute | solution.py:218
  62.5 1.3 %collective-permute-start.14 = (bf16[32,3328]{1,0:T(8,128)(2,1)S(1)}, bf16[32,3328]{1,0:T(8,128)(2,1)S(1)}, u32[]{:S(2)}, u32[]{:S(2)}) collective-permute-start(bf16[32,3328]{1,0:T(8,128)(2,1)S(1)} %get-tuple-element.21), channel_id=1, source_target_pairs={{0,2},{2,0},{4,6},{6,4},{1,3},{3,1},{5,7},{7,5},{8,10},{10,8},{12,... | collective-permute-start | bytes 638984 | tf_op jit(solution)/shard_map/ppermute | solution.py:218
  63.9 0.4 collective-permute-start.15
  64.3 1.8 %collective-permute-start.16 = (bf16[32,3328]{1,0:T(8,128)(2,1)S(1)}, bf16[32,3328]{1,0:T(8,128)(2,1)S(1)}, u32[]{:S(2)}, u32[]{:S(2)}) collective-permute-start(bf16[32,3328]{1,0:T(8,128)(2,1)S(1)} %get-tuple-element.23), channel_id=1, source_target_pairs={{0,6},{2,4},{4,2},{6,0},{1,7},{3,5},{5,3},{7,1},{8,14},{10,12},{12... | collective-permute-start | bytes 638984 | tf_op jit(solution)/shard_map/ppermute | solution.py:218
  66.1 11.8 %shard_map.68 = (bf16[3328,4096]{1,0:T(8,128)(2,1)}, f32[8,128]{1,0:T(8,128)S(1)}) custom-call(s32[1]{0:T(128)} %bitcast.shift_ref, bf16[32,4096]{1,0:T(8,128)(2,1)} %refs_0_.5, bf16[32,4096]{1,0:T(8,128)(2,1)} %copy-done.5, bf16[32,4096]{1,0:T(8,128)(2,1)} %copy-done.6, bf16[32,4096]{1,0:T(8,128)(2,1)} %copy-done.7, bf16[32,4096]{1,0:T(8,128)(2,1)} %copy-done.8, ...), custom_call_target="tpu_custom_call" | custom-call | flops 1 | bytes 1 | tf_op jit(solution)/shard_map/pallas_call | solution.py:157
  77.9 11.8 %collective-permute-done.19.refs_7_ = bf16[32,3328]{1,0:T(8,128)(2,1)S(1)} collective-permute-done((bf16[32,3328]{1,0:T(8,128)(2,1)S(1)}, bf16[32,3328]{1,0:T(8,128)(2,1)S(1)}, u32[]{:S(2)}, u32[]{:S(2)}) %collective-permute-start.19) | collective-permute-done | bytes 213024 | tf_op jit(solution)/shard_map/ppermute | solution.py:218
  89.7 1.9 %collective-permute-done.15.refs_2_ = bf16[32,3328]{1,0:T(8,128)(2,1)S(1)} collective-permute-done((bf16[32,3328]{1,0:T(8,128)(2,1)S(1)}, bf16[32,3328]{1,0:T(8,128)(2,1)S(1)}, u32[]{:S(2)}, u32[]{:S(2)}) %collective-permute-start.15) | collective-permute-done | bytes 213024 | tf_op jit(solution)/shard_map/ppermute | solution.py:218
  91.6 6.6 %collective-permute-done.16.refs_3_ = bf16[32,3328]{1,0:T(8,128)(2,1)S(1)} collective-permute-done((bf16[32,3328]{1,0:T(8,128)(2,1)S(1)}, bf16[32,3328]{1,0:T(8,128)(2,1)S(1)}, u32[]{:S(2)}, u32[]{:S(2)}) %collective-permute-start.16) | collective-permute-done | bytes 213024 | tf_op jit(solution)/shard_map/ppermute | solution.py:218
  98.3 1.4 %shard_map.71 = (bf16[32,6656]{1,0:T(8,128)(2,1)}, bf16[32,6656]{1,0:T(8,128)(2,1)}) custom-call(bf16[32,6656]{1,0:T(8,128)(2,1)S(1)} %copy-done.1, bf16[32,6656]{1,0:T(8,128)(2,1)S(1)} %copy-done.3, f32[32,3328]{1,0:T(8,128)S(1)} %get-tuple-element.20.refs_0_, bf16[32,3328]{1,0:T(8,128)(2,1)S(1)} %collective-permute-done.14.refs_1_, ...), custom_call_target="tpu_custom_call" | custom-call | tf_op jit(solution)/shard_map/pallas_call | solution.py:202
  (51 shorter events, 0.1 us)
Async XLA Ops:
  0.6 12.9 %collective-permute-start.3 = (bf16[32,4096]{1,0:T(8,128)(2,1)}, bf16[32,4096]{1,0:T(8,128)(2,1)S(1)}, u32[]{:S(2)}, u32[]{:S(2)}) collective-permute-start(bf16[32,4096]{1,0:T(8,128)(2,1)} %refs_0_.5), channel_id=1, source_target_pairs={{0,1},{1,0},{2,3},{3,2},{4,5},{5,4},{6,7},{7,6},{8,9},{9,8},{10,11... | collective-permute-start | bytes 786440 | tf_op jit(solution)/shard_map/ppermute | solution.py:218
  3.4 55.9 %copy-start.4 = (bf16[32,3328]{1,0:T(8,128)(2,1)}, bf16[32,3328]{1,0:T(8,128)(2,1)S(1)}, u32[]{:S(2)}) copy-start(bf16[32,3328]{1,0:T(8,128)(2,1)S(1)} %get-tuple-element.17.refs_8_) | copy-start | bytes 638980
  3.4 10.1 %collective-permute-start.10 = (bf16[32,3328]{1,0:T(8,128)(2,1)S(1)}, bf16[32,3328]{1,0:T(8,128)(2,1)S(1)}, u32[]{:S(2)}, u32[]{:S(2)}) collective-permute-start(bf16[32,3328]{1,0:T(8,128)(2,1)S(1)} %get-tuple-element.18), channel_id=1, source_target_pairs={{0,1},{1,0},{2,3},{3,2},{4,5},{5,4},{6,7},{7,6},{8,9},{9,8},{10,11... | collective-permute-start | bytes 638984 | tf_op jit(solution)/shard_map/ppermute | solution.py:218
  5.0 10.1 %collective-permute-start = (bf16[32,4096]{1,0:T(8,128)(2,1)}, bf16[32,4096]{1,0:T(8,128)(2,1)S(1)}, u32[]{:S(2)}, u32[]{:S(2)}) collective-permute-start(bf16[32,4096]{1,0:T(8,128)(2,1)} %refs_0_.5), channel_id=1, source_target_pairs={{0,16},{8,24},{16,0},{24,8},{1,17},{9,25},{17,1},{25,9},{2,18},{10... | collective-permute-start | bytes 786440 | tf_op jit(solution)/shard_map/ppermute | solution.py:218
  6.5 9.1 %collective-permute-start.7 = (bf16[32,3328]{1,0:T(8,128)(2,1)S(1)}, bf16[32,3328]{1,0:T(8,128)(2,1)S(1)}, u32[]{:S(2)}, u32[]{:S(2)}) collective-permute-start(bf16[32,3328]{1,0:T(8,128)(2,1)S(1)} %get-tuple-element.17.refs_8_), channel_id=1, source_target_pairs={{0,4},{2,6},{4,0},{6,2},{1,5},{3,7},{5,1},{7,3},{8,12},{10,14},{12... | collective-permute-start | bytes 638984 | tf_op jit(solution)/shard_map/ppermute | solution.py:218
  6.9 11.7 %collective-permute-start.8 = (bf16[32,3328]{1,0:T(8,128)(2,1)S(1)}, bf16[32,3328]{1,0:T(8,128)(2,1)S(1)}, u32[]{:S(2)}, u32[]{:S(2)}) collective-permute-start(bf16[32,3328]{1,0:T(8,128)(2,1)S(1)} %get-tuple-element.17.refs_8_), channel_id=1, source_target_pairs={{0,2},{2,0},{4,6},{6,4},{1,3},{3,1},{5,7},{7,5},{8,10},{10,8},{12,... | collective-permute-start | bytes 638984 | tf_op jit(solution)/shard_map/ppermute | solution.py:218
  13.5 52.5 %copy-start.16 = (bf16[32,3328]{1,0:T(8,128)(2,1)}, bf16[32,3328]{1,0:T(8,128)(2,1)S(1)}, u32[]{:S(2)}) copy-start(bf16[32,3328]{1,0:T(8,128)(2,1)S(1)} %collective-permute-done.10.refs_12_) | copy-start | bytes 638980
  13.5 6.2 %collective-permute-start.1 = (bf16[32,4096]{1,0:T(8,128)(2,1)}, bf16[32,4096]{1,0:T(8,128)(2,1)S(1)}, u32[]{:S(2)}, u32[]{:S(2)}) collective-permute-start(bf16[32,4096]{1,0:T(8,128)(2,1)} %refs_0_.5), channel_id=1, source_target_pairs={{0,8},{8,0},{16,24},{24,16},{1,9},{9,1},{17,25},{25,17},{2,10},{10... | collective-permute-start | bytes 786440 | tf_op jit(solution)/shard_map/ppermute | solution.py:218
  13.5 32.4 %copy-start.8 = (bf16[32,4096]{1,0:T(8,128)(2,1)}, bf16[32,4096]{1,0:T(8,128)(2,1)S(1)}, u32[]{:S(2)}) copy-start(bf16[32,4096]{1,0:T(8,128)(2,1)S(1)} %collective-permute-done.3.refs_4_.refs_6_) | copy-start | bytes 786436
  13.5 8.7 %collective-permute-start.4 = (bf16[32,4096]{1,0:T(8,128)(2,1)S(1)}, bf16[32,4096]{1,0:T(8,128)(2,1)S(1)}, u32[]{:S(2)}, u32[]{:S(2)}) collective-permute-start(bf16[32,4096]{1,0:T(8,128)(2,1)S(1)} %collective-permute-done.3.refs_4_.refs_6_), channel_id=1, source_target_pairs={{0,16},{8,24},{16,0},{24,8},{1,17},{9,25},{17,1},{25,9},{2,18},{10... | collective-permute-start | bytes 786440 | tf_op jit(solution)/shard_map/ppermute | solution.py:218
  15.1 16.3 %copy-start.5 = (bf16[32,4096]{1,0:T(8,128)(2,1)}, bf16[32,4096]{1,0:T(8,128)(2,1)S(1)}, u32[]{:S(2)}) copy-start(bf16[32,4096]{1,0:T(8,128)(2,1)S(1)} %collective-permute-done.refs_1_) | copy-start | bytes 786436
  15.1 16.3 %collective-permute-start.2 = (bf16[32,4096]{1,0:T(8,128)(2,1)S(1)}, bf16[32,4096]{1,0:T(8,128)(2,1)S(1)}, u32[]{:S(2)}, u32[]{:S(2)}) collective-permute-start(bf16[32,4096]{1,0:T(8,128)(2,1)S(1)} %collective-permute-done.refs_1_), channel_id=1, source_target_pairs={{0,8},{8,0},{16,24},{24,16},{1,9},{9,1},{17,25},{25,17},{2,10},{10... | collective-permute-start | bytes 786440 | tf_op jit(solution)/shard_map/ppermute | solution.py:218
  15.6 30.4 %copy-start.10 = (bf16[32,3328]{1,0:T(8,128)(2,1)}, bf16[32,3328]{1,0:T(8,128)(2,1)S(1)}, u32[]{:S(2)}) copy-start(bf16[32,3328]{1,0:T(8,128)(2,1)S(1)} %collective-permute-done.7.refs_9_.refs_5_) | copy-start | bytes 638980
  15.6 11.1 %collective-permute-start.11 = (bf16[32,3328]{1,0:T(8,128)(2,1)S(1)}, bf16[32,3328]{1,0:T(8,128)(2,1)S(1)}, u32[]{:S(2)}, u32[]{:S(2)}) collective-permute-start(bf16[32,3328]{1,0:T(8,128)(2,1)S(1)} %collective-permute-done.10.refs_12_), channel_id=1, source_target_pairs={{0,4},{2,6},{4,0},{6,2},{1,5},{3,7},{5,1},{7,3},{8,12},{10,14},{12... | collective-permute-start | bytes 638984 | tf_op jit(solution)/shard_map/ppermute | solution.py:218
  18.6 12.9 %copy-start.11 = (bf16[32,3328]{1,0:T(8,128)(2,1)}, bf16[32,3328]{1,0:T(8,128)(2,1)S(1)}, u32[]{:S(2)}) copy-start(bf16[32,3328]{1,0:T(8,128)(2,1)S(1)} %collective-permute-done.8.refs_10_.refs_5_) | copy-start | bytes 638980
  18.6 11.3 %collective-permute-start.12 = (bf16[32,3328]{1,0:T(8,128)(2,1)S(1)}, bf16[32,3328]{1,0:T(8,128)(2,1)S(1)}, u32[]{:S(2)}, u32[]{:S(2)}) collective-permute-start(bf16[32,3328]{1,0:T(8,128)(2,1)S(1)} %collective-permute-done.10.refs_12_), channel_id=1, source_target_pairs={{0,2},{2,0},{4,6},{6,4},{1,3},{3,1},{5,7},{7,5},{8,10},{10,8},{12,... | collective-permute-start | bytes 638984 | tf_op jit(solution)/shard_map/ppermute | solution.py:218
  19.7 11.8 %copy-start.6 = (bf16[32,4096]{1,0:T(8,128)(2,1)}, bf16[32,4096]{1,0:T(8,128)(2,1)S(1)}, u32[]{:S(2)}) copy-start(bf16[32,4096]{1,0:T(8,128)(2,1)S(1)} %collective-permute-done.1.refs_2_) | copy-start | bytes 786436
  19.7 40.2 %collective-permute-start.5 = (bf16[32,4096]{1,0:T(8,128)(2,1)S(1)}, bf16[32,4096]{1,0:T(8,128)(2,1)S(1)}, u32[]{:S(2)}, u32[]{:S(2)}) collective-permute-start(bf16[32,4096]{1,0:T(8,128)(2,1)S(1)} %collective-permute-done.3.refs_4_.refs_6_), channel_id=1, source_target_pairs={{0,8},{8,0},{16,24},{24,16},{1,9},{9,1},{17,25},{25,17},{2,10},{10... | collective-permute-start | bytes 786440 | tf_op jit(solution)/shard_map/ppermute | solution.py:218
  22.3 9.2 %copy-start.9 = (bf16[32,4096]{1,0:T(8,128)(2,1)}, bf16[32,4096]{1,0:T(8,128)(2,1)S(1)}, u32[]{:S(2)}) copy-start(bf16[32,4096]{1,0:T(8,128)(2,1)S(1)} %collective-permute-done.4.refs_5_.refs_8_) | copy-start | bytes 786436
  22.3 42.0 %collective-permute-start.6 = (bf16[32,4096]{1,0:T(8,128)(2,1)S(1)}, bf16[32,4096]{1,0:T(8,128)(2,1)S(1)}, u32[]{:S(2)}, u32[]{:S(2)}) collective-permute-start(bf16[32,4096]{1,0:T(8,128)(2,1)S(1)} %collective-permute-done.4.refs_5_.refs_8_), channel_id=1, source_target_pairs={{0,8},{8,0},{16,24},{24,16},{1,9},{9,1},{17,25},{25,17},{2,10},{10... | collective-permute-start | bytes 786440 | tf_op jit(solution)/shard_map/ppermute | solution.py:218
  26.7 32.7 %collective-permute-start.9 = (bf16[32,3328]{1,0:T(8,128)(2,1)S(1)}, bf16[32,3328]{1,0:T(8,128)(2,1)S(1)}, u32[]{:S(2)}, u32[]{:S(2)}) collective-permute-start(bf16[32,3328]{1,0:T(8,128)(2,1)S(1)} %collective-permute-done.7.refs_9_.refs_5_), channel_id=1, source_target_pairs={{0,2},{2,0},{4,6},{6,4},{1,3},{3,1},{5,7},{7,5},{8,10},{10,8},{12,... | collective-permute-start | bytes 638984 | tf_op jit(solution)/shard_map/ppermute | solution.py:218
  29.8 32.7 %collective-permute-start.13 = (bf16[32,3328]{1,0:T(8,128)(2,1)S(1)}, bf16[32,3328]{1,0:T(8,128)(2,1)S(1)}, u32[]{:S(2)}, u32[]{:S(2)}) collective-permute-start(bf16[32,3328]{1,0:T(8,128)(2,1)S(1)} %collective-permute-done.11.refs_13_.refs_6_), channel_id=1, source_target_pairs={{0,2},{2,0},{4,6},{6,4},{1,3},{3,1},{5,7},{7,5},{8,10},{10,8},{12,... | collective-permute-start | bytes 638984 | tf_op jit(solution)/shard_map/ppermute | solution.py:218
  32.1 66.1 %copy-start.1 = (bf16[32,6656]{1,0:T(8,128)(2,1)S(1)}, bf16[32,6656]{1,0:T(8,128)(2,1)}, u32[]{:S(2)}) copy-start(bf16[32,6656]{1,0:T(8,128)(2,1)} %gate_ref.3) | copy-start | bytes 1277956
  32.1 66.1 %copy-start.3 = (bf16[32,6656]{1,0:T(8,128)(2,1)S(1)}, bf16[32,6656]{1,0:T(8,128)(2,1)}, u32[]{:S(2)}) copy-start(bf16[32,6656]{1,0:T(8,128)(2,1)} %up_ref.3) | copy-start | bytes 1277956
  45.5 18.4 %collective-permute-start.17 = (bf16[32,3328]{1,0:T(8,128)(2,1)S(1)}, bf16[32,3328]{1,0:T(8,128)(2,1)S(1)}, u32[]{:S(2)}, u32[]{:S(2)}) collective-permute-start(bf16[32,3328]{1,0:T(8,128)(2,1)S(1)} %get-tuple-element.25), channel_id=1, source_target_pairs={{0,2},{2,0},{4,6},{6,4},{1,3},{3,1},{5,7},{7,5},{8,10},{10,8},{12,... | collective-permute-start | bytes 638984 | tf_op jit(solution)/shard_map/ppermute | solution.py:218
  59.4 6.6 %copy-start.17 = (bf16[32,3328]{1,0:T(8,128)(2,1)}, bf16[32,3328]{1,0:T(8,128)(2,1)S(1)}, u32[]{:S(2)}) copy-start(bf16[32,3328]{1,0:T(8,128)(2,1)S(1)} %collective-permute-done.9.refs_11_) | copy-start | bytes 638980
  59.4 18.5 %collective-permute-start.18 = (bf16[32,3328]{1,0:T(8,128)(2,1)S(1)}, bf16[32,3328]{1,0:T(8,128)(2,1)S(1)}, u32[]{:S(2)}, u32[]{:S(2)}) collective-permute-start(bf16[32,3328]{1,0:T(8,128)(2,1)S(1)} %get-tuple-element.26), channel_id=1, source_target_pairs={{0,4},{2,6},{4,0},{6,2},{1,5},{3,7},{5,1},{7,3},{8,12},{10,14},{12... | collective-permute-start | bytes 638984 | tf_op jit(solution)/shard_map/ppermute | solution.py:218
  59.9 6.2 %copy-start.14 = (bf16[32,4096]{1,0:T(8,128)(2,1)}, bf16[32,4096]{1,0:T(8,128)(2,1)S(1)}, u32[]{:S(2)}) copy-start(bf16[32,4096]{1,0:T(8,128)(2,1)S(1)} %collective-permute-done.5.refs_6_) | copy-start | bytes 786436
  59.9 29.8 %collective-permute-start.19 = (bf16[32,3328]{1,0:T(8,128)(2,1)S(1)}, bf16[32,3328]{1,0:T(8,128)(2,1)S(1)}, u32[]{:S(2)}, u32[]{:S(2)}) collective-permute-start(bf16[32,3328]{1,0:T(8,128)(2,1)S(1)} %get-tuple-element.27), channel_id=1, source_target_pairs={{0,6},{2,4},{4,2},{6,0},{1,7},{3,5},{5,3},{7,1},{8,14},{10,12},{12... | collective-permute-start | bytes 638984 | tf_op jit(solution)/shard_map/ppermute | solution.py:218
  62.5 27.2 %collective-permute-start.14 = (bf16[32,3328]{1,0:T(8,128)(2,1)S(1)}, bf16[32,3328]{1,0:T(8,128)(2,1)S(1)}, u32[]{:S(2)}, u32[]{:S(2)}) collective-permute-start(bf16[32,3328]{1,0:T(8,128)(2,1)S(1)} %get-tuple-element.21), channel_id=1, source_target_pairs={{0,2},{2,0},{4,6},{6,4},{1,3},{3,1},{5,7},{7,5},{8,10},{10,8},{12,... | collective-permute-start | bytes 638984 | tf_op jit(solution)/shard_map/ppermute | solution.py:218
  63.9 27.8 %collective-permute-start.15 = (bf16[32,3328]{1,0:T(8,128)(2,1)S(1)}, bf16[32,3328]{1,0:T(8,128)(2,1)S(1)}, u32[]{:S(2)}, u32[]{:S(2)}) collective-permute-start(bf16[32,3328]{1,0:T(8,128)(2,1)S(1)} %get-tuple-element.22), channel_id=1, source_target_pairs={{0,4},{2,6},{4,0},{6,2},{1,5},{3,7},{5,1},{7,3},{8,12},{10,14},{12... | collective-permute-start | bytes 638984 | tf_op jit(solution)/shard_map/ppermute | solution.py:218
  64.3 34.0 %collective-permute-start.16 = (bf16[32,3328]{1,0:T(8,128)(2,1)S(1)}, bf16[32,3328]{1,0:T(8,128)(2,1)S(1)}, u32[]{:S(2)}, u32[]{:S(2)}) collective-permute-start(bf16[32,3328]{1,0:T(8,128)(2,1)S(1)} %get-tuple-element.23), channel_id=1, source_target_pairs={{0,6},{2,4},{4,2},{6,0},{1,7},{3,5},{5,3},{7,1},{8,14},{10,12},{12... | collective-permute-start | bytes 638984 | tf_op jit(solution)/shard_map/ppermute | solution.py:218
  (7 other events, 14.4 us)

commit v2 on v1

--- a/solution.py
+++ b/solution.py
@@ -112,7 +112,7 @@
 
 
 def outer_kernel(tok, tile, shift_ref, *refs):
-    out_ref, token, grads, hidden, ready, sems, in_sems = refs[16:]
+    out_ref, token, grads, hidden, ready, sems, in_sems = refs[17:]
     token[...] = jnp.zeros_like(token)
     copies = []
     for half in range(2):
@@ -151,7 +151,7 @@
         copy_out(i).wait()
 
 
-def outer(shift, grads, hidden, tile=128, slots=26):
+def outer(shift, grads, hidden, after, tile=128, slots=26):
     tok, width = grads[0].shape
     rows = hidden[0].shape[1]
     return pl.pallas_call(
@@ -160,7 +160,7 @@
             jax.ShapeDtypeStruct((rows, width), BF16),
             jax.ShapeDtypeStruct((8, 128), F32),
         ],
-        in_specs=[SMEM] + [ANYWHERE] * 16,
+        in_specs=[SMEM] + [ANYWHERE] * 17,
         out_specs=[ANYWHERE, VMEM],
         scratch_shapes=[
             pltpu.VMEM((8 * tok, width), BF16),
@@ -171,7 +171,7 @@
         ],
         compiler_params=pltpu.CompilerParams(vmem_limit_bytes=40 << 20),
         cost_estimate=QUICK,
-    )(shift, *in_hbm(grads), *in_hbm(hidden))
+    )(shift, *in_hbm([*grads, *hidden]), after)
 
 
 def finish(hidden_grad, gate_vals, up_vals):
@@ -183,29 +183,30 @@
     return gate_grad, up_grad
 
 
-def finish_kernel(parts, gate_ref, up_ref, *refs):
-    gate_out, up_out = refs[-2:]
-    at = 0
-    for i in range(parts):
-        p0, r1, r2, r3 = refs[4 * i : 4 * i + 4]
-        columns = slice(at, at + p0.shape[1])
-        total = p0[...] + r1[...].astype(F32) + r2[...].astype(F32) + r3[...].astype(F32)
-        gate_out[:, columns], up_out[:, columns] = finish(
-            total, gate_ref[:, columns].astype(F32), up_ref[:, columns].astype(F32)
-        )
-        at += p0.shape[1]
-
-
-def finished(gate_pre, up_pre, sums, after):
-    vmem = pl.BlockSpec(memory_space=pltpu.VMEM)
-    terms = [term for part in sums for term in part]
+def finish_kernel(gate_ref, up_ref, p0, r1, r2, r3, *refs):
+    gate_out, up_out, token = refs[-3:]
+    total = p0[...] + r1[...].astype(F32) + r2[...].astype(F32) + r3[...].astype(F32)
+    gate_out[...], up_out[...] = finish(
+        total, gate_ref[...].astype(F32), up_ref[...].astype(F32)
+    )
+    token[...] = jnp.zeros_like(token)
+
+
+def finished(gate_pre, up_pre, part, terms, others):
+    tok, width = terms[0].shape
+    here = pl.BlockSpec((tok, width), lambda i: (0, part))
+    term = pl.BlockSpec((tok, width), lambda i: (0, 0))
     return pl.pallas_call(
-        functools.partial(finish_kernel, len(sums)),
-        out_shape=[jax.ShapeDtypeStruct(gate_pre.shape, BF16)] * 2,
-        in_specs=[vmem] * (2 + len(terms)) + [pl.BlockSpec(memory_space=pl.ANY)],
-        out_specs=[vmem, vmem],
+        finish_kernel,
+        grid=(1,),
+        out_shape=[jax.ShapeDtypeStruct(gate_pre.shape, BF16)] * 2
+        + [jax.ShapeDtypeStruct((8, 128), F32)],
+        in_specs=[here, here] + [term] * 4 + [ANYWHERE] * len(others),
+        out_specs=[here, here, pl.BlockSpec((8, 128), lambda i: (0, 0))],
+        input_output_aliases={6: 0, 7: 1} if part else {},
         compiler_params=pltpu.CompilerParams(vmem_limit_bytes=16 << 20),
-    )(gate_pre, up_pre, *terms, after)
+        cost_estimate=QUICK,
+    )(gate_pre, up_pre, *terms, *others)
 
 
 def by_distance(gate_pre, up_pre, out_grad, down_weight):
@@ -243,12 +244,19 @@
         r2, r3, r1 = send(p2, "col", 2), send(p3, "col", 3), send(p1, "col", 1)
         return p0, r1, r2, r3
 
-    after = (own_layer[1], q0)
-    sums = [reduced(partials(shift, grads, down_weight, 0, half, after))]
-    after = (own_layer[2], other_layer[1], other_layer[2], q2)
-    sums.append(reduced(partials(shift, grads, down_weight, half, ff - half, after)))
-    weight_grad, token = outer(shift, grads + (q0, q2, q1, q3), own_layer + other_layer)
-    gate_grad, up_grad = finished(gate_pre, up_pre, sums, token)
+    terms = partials(shift, grads, down_weight, 0, half, (other,))
+    first = reduced(terms)
+    second = reduced(partials(shift, grads, down_weight, half, half, (terms[0], *own_layer[1:3], *other_layer[1:3], q0)))
+    gate_grad, up_grad, token = finished(gate_pre, up_pre, 0, first, ())
+    weight_grad, token = outer(
+        shift,
+        (g0, g2, g1, g3, q0, q2, q1, q3),
+        own_layer + other_layer,
+        token,
+    )
+    gate_grad, up_grad, _ = finished(
+        gate_pre, up_pre, 1, second, (gate_grad, up_grad, token)
+    )
     return weight_grad, gate_grad, up_grad
 
 

time: 100 us -> 84.8 us (0.85)
  the two profiles are of different devices: /device:TPU:18 before, /device:TPU:0 now
where the time goes in v2:
time: 84.8 us; the launch traced here: 84.5 us
  Pallas kernels  40.8 us (48%)
  starting transfers between devices  24.5 us (29%)
  waiting for transfers between devices  14.2 us (17%)
  local copies, waits for them, and re-layouts  4.26 us (5%)
    pallas_call x2, Pallas kernels, partials(): pl.pallas_call(functools.partial(partial_kernel, tok, first, tiles, len(a...  26.8 us
    ppermute x20, starting transfers between devices, send(): return lax.ppermute(x, axis, xor_pairs(lax.axis_size(axis), distance))  24.5 us
    ppermute x20, waiting for transfers between devices, send(): return lax.ppermute(x, axis, xor_pairs(lax.axis_size(axis), distance))  14.2 us
    pallas_call x1, Pallas kernels, outer(): pl.pallas_call(functools.partial(outer_kernel, tok, tile), out_shape=[jax...  11.8 us
    unnamed x42, local copies, waits for them, and re-layouts  4.26 us
    pallas_call x2, Pallas kernels, finished(): pl.pallas_call(finish_kernel, grid=(1,), out_shape=[jax.ShapeDtypeStruct(...  1.99 us
  transfers between devices with their start and end apart: 20, of which 4 were waited for; matrix products, arithmetic and copies ran while one was open for 0% of the time, Pallas kernels for 47%

profile of v2, /device:TPU:0, one launch (start us, length us, event | category | flops | bytes accessed | tf_op | source)
XLA Modules:
  0.0 84.5 jit_solution(11105400105519716552)
XLA Ops:
  0.6 3.0 %collective-permute-start = (bf16[32,4096]{1,0:T(8,128)(2,1)}, bf16[32,4096]{1,0:T(8,128)(2,1)S(1)}, u32[]{:S(2)}, u32[]{:S(2)}) collective-permute-start(bf16[32,4096]{1,0:T(8,128)(2,1)} %refs_0_.5), channel_id=1, source_target_pairs={{0,16},{8,24},{16,0},{24,8},{1,17},{9,25},{17,1},{25,9},{2,18},{10... | collective-permute-start | bytes 786440 | tf_op jit(solution)/shard_map/ppermute | solution.py:219
  3.7 1.0 %copy-done = bf16[32,6656]{1,0:T(8,128)(2,1)S(1)} copy-done((bf16[32,6656]{1,0:T(8,128)(2,1)S(1)}, bf16[32,6656]{1,0:T(8,128)(2,1)}, u32[]{:S(2)}) %copy-start) | copy-done | bytes 426008
  4.7 1.0 %copy-done.2 = bf16[32,6656]{1,0:T(8,128)(2,1)S(1)} copy-done((bf16[32,6656]{1,0:T(8,128)(2,1)S(1)}, bf16[32,6656]{1,0:T(8,128)(2,1)}, u32[]{:S(2)}) %copy-start.2) | copy-done | bytes 426008
  5.7 0.2 shard_map.67
  5.9 1.6 %collective-permute-start.10 = (bf16[32,3328]{1,0:T(8,128)(2,1)S(1)}, bf16[32,3328]{1,0:T(8,128)(2,1)S(1)}, u32[]{:S(2)}, u32[]{:S(2)}) collective-permute-start(bf16[32,3328]{1,0:T(8,128)(2,1)S(1)} %get-tuple-element.21), channel_id=1, source_target_pairs={{0,1},{1,0},{2,3},{3,2},{4,5},{5,4},{6,7},{7,6},{8,9},{9,8},{10,11... | collective-permute-start | bytes 638984 | tf_op jit(solution)/shard_map/ppermute | solution.py:219
  7.4 2.6 %collective-permute-start.7 = (bf16[32,3328]{1,0:T(8,128)(2,1)S(1)}, bf16[32,3328]{1,0:T(8,128)(2,1)S(1)}, u32[]{:S(2)}, u32[]{:S(2)}) collective-permute-start(bf16[32,3328]{1,0:T(8,128)(2,1)S(1)} %get-tuple-element.20.refs_8_), channel_id=1, source_target_pairs={{0,4},{2,6},{4,0},{6,2},{1,5},{3,7},{5,1},{7,3},{8,12},{10,14},{12... | collective-permute-start | bytes 638984 | tf_op jit(solution)/shard_map/ppermute | solution.py:219
  10.0 1.6 %collective-permute-start.8 = (bf16[32,3328]{1,0:T(8,128)(2,1)S(1)}, bf16[32,3328]{1,0:T(8,128)(2,1)S(1)}, u32[]{:S(2)}, u32[]{:S(2)}) collective-permute-start(bf16[32,3328]{1,0:T(8,128)(2,1)S(1)} %get-tuple-element.20.refs_8_), channel_id=1, source_target_pairs={{0,2},{2,0},{4,6},{6,4},{1,3},{3,1},{5,7},{7,5},{8,10},{10,8},{12,... | collective-permute-start | bytes 638984 | tf_op jit(solution)/shard_map/ppermute | solution.py:219
  11.6 1.1 %collective-permute-done.10.refs_5_.refs_12_ = bf16[32,3328]{1,0:T(8,128)(2,1)S(1)} collective-permute-done((bf16[32,3328]{1,0:T(8,128)(2,1)S(1)}, bf16[32,3328]{1,0:T(8,128)(2,1)S(1)}, u32[]{:S(2)}, u32[]{:S(2)}) %collective-permute-start.10) | collective-permute-done | bytes 213024 | tf_op jit(solution)/shard_map/ppermute | solution.py:219
  12.7 1.5 %collective-permute-start.3 = (bf16[32,4096]{1,0:T(8,128)(2,1)}, bf16[32,4096]{1,0:T(8,128)(2,1)S(1)}, u32[]{:S(2)}, u32[]{:S(2)}) collective-permute-start(bf16[32,4096]{1,0:T(8,128)(2,1)} %refs_0_.5), channel_id=1, source_target_pairs={{0,1},{1,0},{2,3},{3,2},{4,5},{5,4},{6,7},{7,6},{8,9},{9,8},{10,11... | collective-permute-start | bytes 786440 | tf_op jit(solution)/shard_map/ppermute | solution.py:219
  14.2 6.5 %collective-permute-done.7.refs_9_.refs_6_ = bf16[32,3328]{1,0:T(8,128)(2,1)S(1)} collective-permute-done((bf16[32,3328]{1,0:T(8,128)(2,1)S(1)}, bf16[32,3328]{1,0:T(8,128)(2,1)S(1)}, u32[]{:S(2)}, u32[]{:S(2)}) %collective-permute-start.7) | collective-permute-done | bytes 213024 | tf_op jit(solution)/shard_map/ppermute | solution.py:219
  20.7 0.2 collective-permute-done.8.refs_10_.refs_7_
  20.9 3.8 %collective-permute-start.12 = (bf16[32,3328]{1,0:T(8,128)(2,1)S(1)}, bf16[32,3328]{1,0:T(8,128)(2,1)S(1)}, u32[]{:S(2)}, u32[]{:S(2)}) collective-permute-start(bf16[32,3328]{1,0:T(8,128)(2,1)S(1)} %collective-permute-done.10.refs_5_.refs_12_), channel_id=1, source_target_pairs={{0,2},{2,0},{4,6},{6,4},{1,3},{3,1},{5,7},{7,5},{8,10},{10,8},{12,... | collective-permute-start | bytes 638984 | tf_op jit(solution)/shard_map/ppermute | solution.py:219
  24.6 0.1 collective-permute-start.9
  24.7 0.5 collective-permute-start.4
  25.3 0.1 copy-done.8
  25.4 0.6 copy-done.9
  26.0 13.3 %shard_map.68 = (f32[32,3328]{1,0:T(8,128)S(1)}, bf16[32,3328]{1,0:T(8,128)(2,1)S(1)}, bf16[32,3328]{1,0:T(8,128)(2,1)S(1)}, bf16[32,3328]{1,0:T(8,128)(2,1)S(1)}) custom-call(s32[1]{0:T(128)} %bitcast.shift_ref, bf16[32,4096]{1,0:T(8,128)(2,1)} %refs_0_.5, bf16[32,4096]{1,0:T(8,128)(2,1)} %copy-done.7, bf16[32,4096]{1,0:T(8,128)(2,1)} %copy-done.8, ...), custom_call_target="tpu_custom_call" | custom-call | flops 1 | bytes 1 | tf_op jit(solution)/shard_map/pallas_call | solution.py:97
  39.3 0.7 copy-done.4
  40.0 1.9 %collective-permute-start.14 = (bf16[32,3328]{1,0:T(8,128)(2,1)S(1)}, bf16[32,3328]{1,0:T(8,128)(2,1)S(1)}, u32[]{:S(2)}, u32[]{:S(2)}) collective-permute-start(bf16[32,3328]{1,0:T(8,128)(2,1)S(1)} %get-tuple-element.23), channel_id=1, source_target_pairs={{0,2},{2,0},{4,6},{6,4},{1,3},{3,1},{5,7},{7,5},{8,10},{10,8},{12,... | collective-permute-start | bytes 638984 | tf_op jit(solution)/shard_map/ppermute | solution.py:219
  42.0 0.1 collective-permute-start.15
  42.1 2.4 %collective-permute-start.16 = (bf16[32,3328]{1,0:T(8,128)(2,1)S(1)}, bf16[32,3328]{1,0:T(8,128)(2,1)S(1)}, u32[]{:S(2)}, u32[]{:S(2)}) collective-permute-start(bf16[32,3328]{1,0:T(8,128)(2,1)S(1)} %get-tuple-element.25), channel_id=1, source_target_pairs={{0,6},{2,4},{4,2},{6,0},{1,7},{3,5},{5,3},{7,1},{8,14},{10,12},{12... | collective-permute-start | bytes 638984 | tf_op jit(solution)/shard_map/ppermute | solution.py:219
  44.5 13.5 %shard_map.71 = (f32[32,3328]{1,0:T(8,128)S(1)}, bf16[32,3328]{1,0:T(8,128)(2,1)S(1)}, bf16[32,3328]{1,0:T(8,128)(2,1)S(1)}, bf16[32,3328]{1,0:T(8,128)(2,1)S(1)}) custom-call(s32[1]{0:T(128)} %bitcast.shift_ref, bf16[32,4096]{1,0:T(8,128)(2,1)} %refs_0_.5, bf16[32,4096]{1,0:T(8,128)(2,1)} %copy-done.7, bf16[32,4096]{1,0:T(8,128)(2,1)} %copy-done.8, ...), custom_call_target="tpu_custom_call" | custom-call | flops 1 | bytes 1 | tf_op jit(solution)/shard_map/pallas_call | solution.py:97
  58.0 1.1 %collective-permute-start.13 = (bf16[32,3328]{1,0:T(8,128)(2,1)}, bf16[32,3328]{1,0:T(8,128)(2,1)S(1)}, u32[]{:S(2)}, u32[]{:S(2)}) collective-permute-start(bf16[32,3328]{1,0:T(8,128)(2,1)} %copy-done.14), channel_id=1, source_target_pairs={{0,2},{2,0},{4,6},{6,4},{1,3},{3,1},{5,7},{7,5},{8,10},{10,8},{12,... | collective-permute-start | bytes 638984 | tf_op jit(solution)/shard_map/ppermute | solution.py:219
  59.1 1.0 %collective-permute-start.17 = (bf16[32,3328]{1,0:T(8,128)(2,1)S(1)}, bf16[32,3328]{1,0:T(8,128)(2,1)S(1)}, u32[]{:S(2)}, u32[]{:S(2)}) collective-permute-start(bf16[32,3328]{1,0:T(8,128)(2,1)S(1)} %get-tuple-element.29), channel_id=1, source_target_pairs={{0,2},{2,0},{4,6},{6,4},{1,3},{3,1},{5,7},{7,5},{8,10},{10,8},{12,... | collective-permute-start | bytes 638984 | tf_op jit(solution)/shard_map/ppermute | solution.py:219
  60.1 0.5 collective-permute-start.18
  60.6 2.9 %collective-permute-start.19 = (bf16[32,3328]{1,0:T(8,128)(2,1)S(1)}, bf16[32,3328]{1,0:T(8,128)(2,1)S(1)}, u32[]{:S(2)}, u32[]{:S(2)}) collective-permute-start(bf16[32,3328]{1,0:T(8,128)(2,1)S(1)} %get-tuple-element.31), channel_id=1, source_target_pairs={{0,6},{2,4},{4,2},{6,0},{1,7},{3,5},{5,3},{7,1},{8,14},{10,12},{12... | collective-permute-start | bytes 638984 | tf_op jit(solution)/shard_map/ppermute | solution.py:219
  63.5 1.0 %shard_map.69 = (bf16[32,6656]{1,0:T(8,128)(2,1)}, bf16[32,6656]{1,0:T(8,128)(2,1)}, f32[8,128]{1,0:T(8,128)S(1)}) custom-call(bf16[32,6656]{1,0:T(8,128)(2,1)S(1)} %copy-done.1, bf16[32,6656]{1,0:T(8,128)(2,1)S(1)} %copy-done.3, f32[32,3328]{1,0:T(8,128)S(1)} %copy-done.5, bf16[32,3328]{1,0:T(8,128)(2,1)S(1)} %collective-permute-done.14.r1, ...), custom_call_target="tpu_custom_call" | custom-call | flops 1 | bytes 1 | tf_op jit(solution)/shard_map/pallas_call | solution.py:199
  64.5 6.4 %collective-permute-done.13.refs_15_ = bf16[32,3328]{1,0:T(8,128)(2,1)S(1)} collective-permute-done((bf16[32,3328]{1,0:T(8,128)(2,1)}, bf16[32,3328]{1,0:T(8,128)(2,1)S(1)}, u32[]{:S(2)}, u32[]{:S(2)}) %collective-permute-start.13) | collective-permute-done | bytes 213024 | tf_op jit(solution)/shard_map/ppermute | solution.py:219
  70.9 0.6 copy-done.20
  71.6 0.1 copy-done.18
  71.7 11.8 %shard_map.70 = (bf16[3328,4096]{1,0:T(8,128)(2,1)}, f32[8,128]{1,0:T(8,128)S(1)}) custom-call(s32[1]{0:T(128)} %bitcast.shift_ref, bf16[32,4096]{1,0:T(8,128)(2,1)} %refs_0_.5, bf16[32,4096]{1,0:T(8,128)(2,1)} %copy-done.7, bf16[32,4096]{1,0:T(8,128)(2,1)} %copy-done.8, bf16[32,4096]{1,0:T(8,128)(2,1)} %copy-done.9, bf16[32,4096]{1,0:T(8,128)(2,1)} %copy-done.10, ...), custom_call_target="tpu_custom_call" | custom-call | flops 1 | bytes 1 | tf_op jit(solution)/shard_map/pallas_call | solution.py:157
  83.5 1.0 %shard_map.72 = (bf16[32,6656]{1,0:T(8,128)(2,1)}, bf16[32,6656]{1,0:T(8,128)(2,1)}, f32[8,128]{1,0:T(8,128)}) custom-call(bf16[32,6656]{1,0:T(8,128)(2,1)S(1)} %copy-done.1, bf16[32,6656]{1,0:T(8,128)(2,1)S(1)} %copy-done.3, f32[32,3328]{1,0:T(8,128)S(1)} %get-tuple-element.28.p0, ...), custom_call_target="tpu_custom_call", output_to_operand_aliasing={{0}: (6, {}), {1}: (7, {})} | custom-call | flops 1 | bytes 1 | tf_op jit(solution)/shard_map/pallas_call | solution.py:199
  (56 shorter events, 0.1 us)
Async XLA Ops:
  0.6 13.5 %collective-permute-start = (bf16[32,4096]{1,0:T(8,128)(2,1)}, bf16[32,4096]{1,0:T(8,128)(2,1)S(1)}, u32[]{:S(2)}, u32[]{:S(2)}) collective-permute-start(bf16[32,4096]{1,0:T(8,128)(2,1)} %refs_0_.5), channel_id=1, source_target_pairs={{0,16},{8,24},{16,0},{24,8},{1,17},{9,25},{17,1},{25,9},{2,18},{10... | collective-permute-start | bytes 786440 | tf_op jit(solution)/shard_map/ppermute | solution.py:219
  5.9 52.1 %copy-start.6 = (bf16[32,3328]{1,0:T(8,128)(2,1)}, bf16[32,3328]{1,0:T(8,128)(2,1)S(1)}, u32[]{:S(2)}) copy-start(bf16[32,3328]{1,0:T(8,128)(2,1)S(1)} %get-tuple-element.20.refs_8_) | copy-start | bytes 638980
  5.9 6.8 %collective-permute-start.10 = (bf16[32,3328]{1,0:T(8,128)(2,1)S(1)}, bf16[32,3328]{1,0:T(8,128)(2,1)S(1)}, u32[]{:S(2)}, u32[]{:S(2)}) collective-permute-start(bf16[32,3328]{1,0:T(8,128)(2,1)S(1)} %get-tuple-element.21), channel_id=1, source_target_pairs={{0,1},{1,0},{2,3},{3,2},{4,5},{5,4},{6,7},{7,6},{8,9},{9,8},{10,11... | collective-permute-start | bytes 638984 | tf_op jit(solution)/shard_map/ppermute | solution.py:219
  7.4 17.2 %collective-permute-start.1 = (bf16[32,4096]{1,0:T(8,128)(2,1)}, bf16[32,4096]{1,0:T(8,128)(2,1)S(1)}, u32[]{:S(2)}, u32[]{:S(2)}) collective-permute-start(bf16[32,4096]{1,0:T(8,128)(2,1)} %refs_0_.5), channel_id=1, source_target_pairs={{0,8},{8,0},{16,24},{24,16},{1,9},{9,1},{17,25},{25,17},{2,10},{10... | collective-permute-start | bytes 786440 | tf_op jit(solution)/shard_map/ppermute | solution.py:219
  7.4 13.2 %collective-permute-start.7 = (bf16[32,3328]{1,0:T(8,128)(2,1)S(1)}, bf16[32,3328]{1,0:T(8,128)(2,1)S(1)}, u32[]{:S(2)}, u32[]{:S(2)}) collective-permute-start(bf16[32,3328]{1,0:T(8,128)(2,1)S(1)} %get-tuple-element.20.refs_8_), channel_id=1, source_target_pairs={{0,4},{2,6},{4,0},{6,2},{1,5},{3,7},{5,1},{7,3},{8,12},{10,14},{12... | collective-permute-start | bytes 638984 | tf_op jit(solution)/shard_map/ppermute | solution.py:219
  10.0 10.8 %collective-permute-start.8 = (bf16[32,3328]{1,0:T(8,128)(2,1)S(1)}, bf16[32,3328]{1,0:T(8,128)(2,1)S(1)}, u32[]{:S(2)}, u32[]{:S(2)}) collective-permute-start(bf16[32,3328]{1,0:T(8,128)(2,1)S(1)} %get-tuple-element.20.refs_8_), channel_id=1, source_target_pairs={{0,2},{2,0},{4,6},{6,4},{1,3},{3,1},{5,7},{7,5},{8,10},{10,8},{12,... | collective-permute-start | bytes 638984 | tf_op jit(solution)/shard_map/ppermute | solution.py:219
  12.7 12.6 %copy-start.11 = (bf16[32,3328]{1,0:T(8,128)(2,1)}, bf16[32,3328]{1,0:T(8,128)(2,1)S(1)}, u32[]{:S(2)}) copy-start(bf16[32,3328]{1,0:T(8,128)(2,1)S(1)} %collective-permute-done.10.refs_5_.refs_12_) | copy-start | bytes 638980
  12.7 12.1 %collective-permute-start.3 = (bf16[32,4096]{1,0:T(8,128)(2,1)}, bf16[32,4096]{1,0:T(8,128)(2,1)S(1)}, u32[]{:S(2)}, u32[]{:S(2)}) collective-permute-start(bf16[32,4096]{1,0:T(8,128)(2,1)} %refs_0_.5), channel_id=1, source_target_pairs={{0,1},{1,0},{2,3},{3,2},{4,5},{5,4},{6,7},{7,6},{8,9},{9,8},{10,11... | collective-permute-start | bytes 786440 | tf_op jit(solution)/shard_map/ppermute | solution.py:219
  14.2 11.1 %copy-start.7 = (bf16[32,4096]{1,0:T(8,128)(2,1)}, bf16[32,4096]{1,0:T(8,128)(2,1)S(1)}, u32[]{:S(2)}) copy-start(bf16[32,4096]{1,0:T(8,128)(2,1)S(1)} %collective-permute-done.refs_1_) | copy-start | bytes 786436
  14.2 11.1 %collective-permute-start.2 = (bf16[32,4096]{1,0:T(8,128)(2,1)S(1)}, bf16[32,4096]{1,0:T(8,128)(2,1)S(1)}, u32[]{:S(2)}, u32[]{:S(2)}) collective-permute-start(bf16[32,4096]{1,0:T(8,128)(2,1)S(1)} %collective-permute-done.refs_1_), channel_id=1, source_target_pairs={{0,8},{8,0},{16,24},{24,16},{1,9},{9,1},{17,25},{25,17},{2,10},{10... | collective-permute-start | bytes 786440 | tf_op jit(solution)/shard_map/ppermute | solution.py:219
  20.7 23.8 %copy-start.12 = (bf16[32,3328]{1,0:T(8,128)(2,1)}, bf16[32,3328]{1,0:T(8,128)(2,1)S(1)}, u32[]{:S(2)}) copy-start(bf16[32,3328]{1,0:T(8,128)(2,1)S(1)} %collective-permute-done.7.refs_9_.refs_6_) | copy-start | bytes 638980
  20.7 19.4 %collective-permute-start.11 = (bf16[32,3328]{1,0:T(8,128)(2,1)S(1)}, bf16[32,3328]{1,0:T(8,128)(2,1)S(1)}, u32[]{:S(2)}, u32[]{:S(2)}) collective-permute-start(bf16[32,3328]{1,0:T(8,128)(2,1)S(1)} %collective-permute-done.10.refs_5_.refs_12_), channel_id=1, source_target_pairs={{0,4},{2,6},{4,0},{6,2},{1,5},{3,7},{5,1},{7,3},{8,12},{10,14},{12... | collective-permute-start | bytes 638984 | tf_op jit(solution)/shard_map/ppermute | solution.py:219
  20.9 23.6 %copy-start.13 = (bf16[32,3328]{1,0:T(8,128)(2,1)}, bf16[32,3328]{1,0:T(8,128)(2,1)S(1)}, u32[]{:S(2)}) copy-start(bf16[32,3328]{1,0:T(8,128)(2,1)S(1)} %collective-permute-done.8.refs_10_.refs_7_) | copy-start | bytes 638980
  20.9 21.1 %collective-permute-start.12 = (bf16[32,3328]{1,0:T(8,128)(2,1)S(1)}, bf16[32,3328]{1,0:T(8,128)(2,1)S(1)}, u32[]{:S(2)}, u32[]{:S(2)}) collective-permute-start(bf16[32,3328]{1,0:T(8,128)(2,1)S(1)} %collective-permute-done.10.refs_5_.refs_12_), channel_id=1, source_target_pairs={{0,2},{2,0},{4,6},{6,4},{1,3},{3,1},{5,7},{7,5},{8,10},{10,8},{12,... | collective-permute-start | bytes 638984 | tf_op jit(solution)/shard_map/ppermute | solution.py:219
  24.6 17.4 %collective-permute-start.9 = (bf16[32,3328]{1,0:T(8,128)(2,1)S(1)}, bf16[32,3328]{1,0:T(8,128)(2,1)S(1)}, u32[]{:S(2)}, u32[]{:S(2)}) collective-permute-start(bf16[32,3328]{1,0:T(8,128)(2,1)S(1)} %collective-permute-done.7.refs_9_.refs_6_), channel_id=1, source_target_pairs={{0,2},{2,0},{4,6},{6,4},{1,3},{3,1},{5,7},{7,5},{8,10},{10,8},{12,... | collective-permute-start | bytes 638984 | tf_op jit(solution)/shard_map/ppermute | solution.py:219
  24.7 19.8 %copy-start.10 = (bf16[32,4096]{1,0:T(8,128)(2,1)}, bf16[32,4096]{1,0:T(8,128)(2,1)S(1)}, u32[]{:S(2)}) copy-start(bf16[32,4096]{1,0:T(8,128)(2,1)S(1)} %collective-permute-done.3.refs_4_.refs_10_) | copy-start | bytes 786436
  24.7 19.7 %collective-permute-start.4 = (bf16[32,4096]{1,0:T(8,128)(2,1)S(1)}, bf16[32,4096]{1,0:T(8,128)(2,1)S(1)}, u32[]{:S(2)}, u32[]{:S(2)}) collective-permute-start(bf16[32,4096]{1,0:T(8,128)(2,1)S(1)} %collective-permute-done.3.refs_4_.refs_10_), channel_id=1, source_target_pairs={{0,16},{8,24},{16,0},{24,8},{1,17},{9,25},{17,1},{25,9},{2,18},{10... | collective-permute-start | bytes 786440 | tf_op jit(solution)/shard_map/ppermute | solution.py:219
  25.2 32.8 %collective-permute-start.5 = (bf16[32,4096]{1,0:T(8,128)(2,1)S(1)}, bf16[32,4096]{1,0:T(8,128)(2,1)S(1)}, u32[]{:S(2)}, u32[]{:S(2)}) collective-permute-start(bf16[32,4096]{1,0:T(8,128)(2,1)S(1)} %collective-permute-done.3.refs_4_.refs_10_), channel_id=1, source_target_pairs={{0,8},{8,0},{16,24},{24,16},{1,9},{9,1},{17,25},{25,17},{2,10},{10... | collective-permute-start | bytes 786440 | tf_op jit(solution)/shard_map/ppermute | solution.py:219
  26.0 37.5 %copy-start.1 = (bf16[32,6656]{1,0:T(8,128)(2,1)S(1)}, bf16[32,6656]{1,0:T(8,128)(2,1)}, u32[]{:S(2)}) copy-start(bf16[32,6656]{1,0:T(8,128)(2,1)} %gate_ref.5) | copy-start | bytes 1277956
  26.0 37.5 %copy-start.3 = (bf16[32,6656]{1,0:T(8,128)(2,1)S(1)}, bf16[32,6656]{1,0:T(8,128)(2,1)}, u32[]{:S(2)}) copy-start(bf16[32,6656]{1,0:T(8,128)(2,1)} %up_ref.5) | copy-start | bytes 1277956
  40.0 23.5 %copy-start.5 = (f32[32,3328]{1,0:T(8,128)S(1)}, f32[32,3328]{1,0:T(8,128)}, u32[]{:S(2)}) copy-start(f32[32,3328]{1,0:T(8,128)} %copy-done.4) | copy-start | bytes 1277956
  40.0 19.1 %collective-permute-start.14 = (bf16[32,3328]{1,0:T(8,128)(2,1)S(1)}, bf16[32,3328]{1,0:T(8,128)(2,1)S(1)}, u32[]{:S(2)}, u32[]{:S(2)}) collective-permute-start(bf16[32,3328]{1,0:T(8,128)(2,1)S(1)} %get-tuple-element.23), channel_id=1, source_target_pairs={{0,2},{2,0},{4,6},{6,4},{1,3},{3,1},{5,7},{7,5},{8,10},{10,8},{12,... | collective-permute-start | bytes 638984 | tf_op jit(solution)/shard_map/ppermute | solution.py:219
  42.0 18.1 %collective-permute-start.15 = (bf16[32,3328]{1,0:T(8,128)(2,1)S(1)}, bf16[32,3328]{1,0:T(8,128)(2,1)S(1)}, u32[]{:S(2)}, u32[]{:S(2)}) collective-permute-start(bf16[32,3328]{1,0:T(8,128)(2,1)S(1)} %get-tuple-element.24), channel_id=1, source_target_pairs={{0,4},{2,6},{4,0},{6,2},{1,5},{3,7},{5,1},{7,3},{8,12},{10,14},{12... | collective-permute-start | bytes 638984 | tf_op jit(solution)/shard_map/ppermute | solution.py:219
  42.1 28.8 %copy-start.19 = (bf16[32,3328]{1,0:T(8,128)(2,1)}, bf16[32,3328]{1,0:T(8,128)(2,1)S(1)}, u32[]{:S(2)}) copy-start(bf16[32,3328]{1,0:T(8,128)(2,1)S(1)} %collective-permute-done.9.refs_11_) | copy-start | bytes 638980
  42.1 18.6 %collective-permute-start.16 = (bf16[32,3328]{1,0:T(8,128)(2,1)S(1)}, bf16[32,3328]{1,0:T(8,128)(2,1)S(1)}, u32[]{:S(2)}, u32[]{:S(2)}) collective-permute-start(bf16[32,3328]{1,0:T(8,128)(2,1)S(1)} %get-tuple-element.25), channel_id=1, source_target_pairs={{0,6},{2,4},{4,2},{6,0},{1,7},{3,5},{5,3},{7,1},{8,14},{10,12},{12... | collective-permute-start | bytes 638984 | tf_op jit(solution)/shard_map/ppermute | solution.py:219
  44.5 26.5 %copy-start.16 = (bf16[32,4096]{1,0:T(8,128)(2,1)}, bf16[32,4096]{1,0:T(8,128)(2,1)S(1)}, u32[]{:S(2)}) copy-start(bf16[32,4096]{1,0:T(8,128)(2,1)S(1)} %collective-permute-done.4.refs_5_) | copy-start | bytes 786436
  44.5 26.5 %collective-permute-start.6 = (bf16[32,4096]{1,0:T(8,128)(2,1)S(1)}, bf16[32,4096]{1,0:T(8,128)(2,1)S(1)}, u32[]{:S(2)}, u32[]{:S(2)}) collective-permute-start(bf16[32,4096]{1,0:T(8,128)(2,1)S(1)} %collective-permute-done.4.refs_5_), channel_id=1, source_target_pairs={{0,8},{8,0},{16,24},{24,16},{1,9},{9,1},{17,25},{25,17},{2,10},{10... | collective-permute-start | bytes 786440 | tf_op jit(solution)/shard_map/ppermute | solution.py:219
  58.0 12.9 %copy-start.17 = (bf16[32,4096]{1,0:T(8,128)(2,1)}, bf16[32,4096]{1,0:T(8,128)(2,1)S(1)}, u32[]{:S(2)}) copy-start(bf16[32,4096]{1,0:T(8,128)(2,1)S(1)} %collective-permute-done.5.refs_6_) | copy-start | bytes 786436
  58.0 12.9 %collective-permute-start.13 = (bf16[32,3328]{1,0:T(8,128)(2,1)}, bf16[32,3328]{1,0:T(8,128)(2,1)S(1)}, u32[]{:S(2)}, u32[]{:S(2)}) collective-permute-start(bf16[32,3328]{1,0:T(8,128)(2,1)} %copy-done.14), channel_id=1, source_target_pairs={{0,2},{2,0},{4,6},{6,4},{1,3},{3,1},{5,7},{7,5},{8,10},{10,8},{12,... | collective-permute-start | bytes 638984 | tf_op jit(solution)/shard_map/ppermute | solution.py:219
  59.1 24.4 %collective-permute-start.17 = (bf16[32,3328]{1,0:T(8,128)(2,1)S(1)}, bf16[32,3328]{1,0:T(8,128)(2,1)S(1)}, u32[]{:S(2)}, u32[]{:S(2)}) collective-permute-start(bf16[32,3328]{1,0:T(8,128)(2,1)S(1)} %get-tuple-element.29), channel_id=1, source_target_pairs={{0,2},{2,0},{4,6},{6,4},{1,3},{3,1},{5,7},{7,5},{8,10},{10,8},{12,... | collective-permute-start | bytes 638984 | tf_op jit(solution)/shard_map/ppermute | solution.py:219
  60.1 23.4 %collective-permute-start.18 = (bf16[32,3328]{1,0:T(8,128)(2,1)S(1)}, bf16[32,3328]{1,0:T(8,128)(2,1)S(1)}, u32[]{:S(2)}, u32[]{:S(2)}) collective-permute-start(bf16[32,3328]{1,0:T(8,128)(2,1)S(1)} %get-tuple-element.30), channel_id=1, source_target_pairs={{0,4},{2,6},{4,0},{6,2},{1,5},{3,7},{5,1},{7,3},{8,12},{10,14},{12... | collective-permute-start | bytes 638984 | tf_op jit(solution)/shard_map/ppermute | solution.py:219
  60.6 22.9 %collective-permute-start.19 = (bf16[32,3328]{1,0:T(8,128)(2,1)S(1)}, bf16[32,3328]{1,0:T(8,128)(2,1)S(1)}, u32[]{:S(2)}, u32[]{:S(2)}) collective-permute-start(bf16[32,3328]{1,0:T(8,128)(2,1)S(1)} %get-tuple-element.31), channel_id=1, source_target_pairs={{0,6},{2,4},{4,2},{6,0},{1,7},{3,5},{5,3},{7,1},{8,14},{10,12},{12... | collective-permute-start | bytes 638984 | tf_op jit(solution)/shard_map/ppermute | solution.py:219
  (9 other events, 12.6 us)

commit v3 on v1

--- a/solution.py
+++ b/solution.py
@@ -12,40 +12,70 @@
 F32 = jnp.float32
 
 
+def of_bytes(n):
+    return pl.CostEstimate(flops=1, bytes_accessed=n, transcendentals=0)
+
+
 def xor_pairs(size, distance):
     return [(i, i ^ distance) for i in range(size)]
 
 
-def block_copies(shift, refs, scratch, base, tok, sems):
+def block_copies(shift, pairs, scratch, base, sems):
+    tok = pairs[0].shape[0] // 2
     copies = []
-    for i, (value, ref) in enumerate(zip((0, 2, 1, 3), refs)):
+    for value in range(4):
+        ref = pairs[value % 2].at[pl.ds(value // 2 * tok, tok)]
         start = pl.multiple_of(base + jnp.bitwise_xor(shift, value) * tok, tok)
         copies.append(
-            pltpu.make_async_copy(ref, scratch.at[pl.ds(start, tok)], sems.at[i])
+            pltpu.make_async_copy(ref, scratch.at[pl.ds(start, tok)], sems.at[value])
         )
     return copies
 
 
-def hidden_kernel(depth_ref, gate_ref, up_ref, mine, theirs):
+def in_hbm(arrays):
+    return [pltpu.with_memory_space_constraint(x, pltpu.HBM) for x in arrays]
+
+
+ANYWHERE = pl.BlockSpec(memory_space=pl.ANY)
+VMEM = pl.BlockSpec(memory_space=pltpu.VMEM)
+SMEM = pl.BlockSpec(memory_space=pltpu.SMEM)
+
+
+def hidden_kernel(
+    depth_ref, gate_ref, up_ref, og_ref, mine, theirs, og_out, gates, ups, sems, og_sem
+):
     half = mine.shape[1]
-    for ref, at in ((mine, depth_ref[0]), (theirs, 1 - depth_ref[0])):
+    copies = []
+    for i, at in enumerate((1 - depth_ref[0], depth_ref[0])):
         columns = pl.ds(pl.multiple_of(at * half, 128), half)
-        gate = gate_ref[:, columns].astype(F32)
-        up = up_ref[:, columns].astype(F32)
-        ref[...] = (gate * jax.nn.sigmoid(gate) * up).astype(ref.dtype)
-
-
-def hidden_halves(depth, gate_pre, up_pre):
+        for j, (src, dst) in enumerate(((gate_ref, gates), (up_ref, ups))):
+            copies.append(
+                pltpu.make_async_copy(src.at[:, columns], dst.at[i], sems.at[i, j])
+            )
+    passed = pltpu.make_async_copy(og_ref, og_out, og_sem)
+    for copy in copies + [passed]:
+        copy.start()
+    for i, out in enumerate((theirs, mine)):
+        copies[2 * i].wait()
+        copies[2 * i + 1].wait()
+        gate = gates[i].astype(F32)
+        out[...] = (gate * jax.nn.sigmoid(gate) * ups[i].astype(F32)).astype(out.dtype)
+    passed.wait()
+
+
+def hidden_halves(depth, gate_pre, up_pre, out_grad):
     tok, ff = gate_pre.shape
-    vmem = pl.BlockSpec(memory_space=pltpu.VMEM)
     return pl.pallas_call(
         hidden_kernel,
-        out_shape=[jax.ShapeDtypeStruct((tok, ff // 2), BF16)] * 2,
-        in_specs=[pl.BlockSpec(memory_space=pltpu.SMEM), vmem, vmem],
-        out_specs=[vmem, vmem],
-        compiler_params=pltpu.CompilerParams(vmem_limit_bytes=8 << 20),
+        out_shape=[jax.ShapeDtypeStruct((tok, ff // 2), BF16)] * 2
+        + [jax.ShapeDtypeStruct(out_grad.shape, BF16)],
+        in_specs=[SMEM] + [ANYWHERE] * 3,
+        out_specs=[VMEM, VMEM, VMEM],
+        scratch_shapes=[pltpu.VMEM((2, tok, ff // 2), BF16)] * 2
+        + [pltpu.SemaphoreType.DMA((2, 2)), pltpu.SemaphoreType.DMA],
+        compiler_params=pltpu.CompilerParams(vmem_limit_bytes=16 << 20),
         cost_estimate=QUICK,
-    )(depth, gate_pre, up_pre)
+    )(depth, *in_hbm([gate_pre, up_pre, out_grad]))
 
 
 def cuts(rows, most):
@@ -54,30 +84,50 @@
     return [(at, min(step, rows - at)) for at in range(0, rows, step)]
 
 
-def in_hbm(arrays):
-    return [pltpu.with_memory_space_constraint(x, pltpu.HBM) for x in arrays]
-
-
-ANYWHERE = pl.BlockSpec(memory_space=pl.ANY)
-VMEM = pl.BlockSpec(memory_space=pltpu.VMEM)
-SMEM = pl.BlockSpec(memory_space=pltpu.SMEM)
-
-
-def partial_kernel(tok, first, tiles, n_after, shift_ref, *refs):
-    grads_in, w_ref, refs = refs[:4], refs[4], refs[5 + n_after :]
+def stack_kernel(*refs):
+    ins, outs, sems = refs[:4], refs[4:6], refs[6]
+    tok = ins[0].shape[0]
+    copies = [
+        pltpu.make_async_copy(
+            ref, outs[i // 2].at[pl.ds(i % 2 * tok, tok)], sems.at[i]
+        )
+        for i, ref in enumerate(ins)
+    ]
+    for copy in copies:
+        copy.start()
+    for copy in copies:
+        copy.wait()
+
+
+def stacked(g0, g2, mine, other):
+    tok = g0.shape[0]
+    return pl.pallas_call(
+        stack_kernel,
+        out_shape=[
+            jax.ShapeDtypeStruct((2 * tok, g0.shape[1]), BF16),
+            jax.ShapeDtypeStruct((2 * tok, mine.shape[1]), BF16),
+        ],
+        in_specs=[ANYWHERE] * 4,
+        out_specs=[VMEM] * 2,
+        scratch_shapes=[pltpu.SemaphoreType.DMA((4,))],
+        cost_estimate=QUICK,
+    )(*in_hbm([g0, g2, mine, other]))
+
+
+def partial_kernel(tok, first, tiles, shift_ref, pair, cores, w_ref, *refs):
     terms_out, (grads, rows, sems, w_sems) = refs[:4], refs[4:]
-    copies = block_copies(shift_ref[0], grads_in, grads, 0, tok, sems)
     fetches = [
         pltpu.make_async_copy(
             w_ref.at[pl.ds(first + at, size)], rows.at[pl.ds(at, size)], w_sems.at[i]
         )
         for i, (at, size) in enumerate(tiles)
     ]
-    for copy in copies:
+    copies = block_copies(shift_ref[0], (pair, cores), grads, 0, sems)
+    for copy in copies + fetches[:1]:
         copy.start()
     for copy in copies:
         copy.wait()
-    for fetch in fetches:
+    for fetch in fetches[1:]:
         fetch.start()
     for fetch, (at, size) in zip(fetches, tiles):
         fetch.wait()
@@ -91,14 +141,14 @@
             ref[:, at : at + size] = terms[k * tok : (k + 1) * tok].astype(ref.dtype)
 
 
-def partials(shift, grads, weight, first, rows, after):
-    tok, width = grads[0].shape
+def partials(shift, pairs, weight, first, rows):
+    tok, width = pairs[0].shape[0] // 2, pairs[0].shape[1]
     tiles = [(0, 256)] + [(256 + at, size) for at, size in cuts(rows - 256, 512)]
     return pl.pallas_call(
-        functools.partial(partial_kernel, tok, first, tiles, len(after)),
+        functools.partial(partial_kernel, tok, first, tiles),
         out_shape=[jax.ShapeDtypeStruct((tok, rows), F32)]
         + [jax.ShapeDtypeStruct((tok, rows), BF16)] * 3,
-        in_specs=[SMEM] + [ANYWHERE] * (5 + len(after)),
+        in_specs=[SMEM] + [ANYWHERE] * 3,
         out_specs=[VMEM] * 4,
         scratch_shapes=[
             pltpu.VMEM((4 * tok, width), BF16),
@@ -107,23 +157,27 @@
             pltpu.SemaphoreType.DMA((len(tiles),)),
         ],
         compiler_params=pltpu.CompilerParams(vmem_limit_bytes=40 << 20),
-        cost_estimate=QUICK,
-    )(shift, *in_hbm([*grads, weight, *after]))
+        cost_estimate=of_bytes(2 * rows * width),
+    )(shift, *pairs, *in_hbm([weight]))
 
 
 def outer_kernel(tok, tile, shift_ref, *refs):
-    out_ref, token, grads, hidden, ready, sems, in_sems = refs[16:]
+    out_ref, token, grads, hidden, ready, sems, in_sems = refs[8:]
     token[...] = jnp.zeros_like(token)
     copies = []
     for half in range(2):
-        base = 4 * tok * half
+        pairs = refs[2 * half : 2 * half + 2]
         copies += block_copies(
-            shift_ref[0], refs[4 * half : 4 * half + 4], grads, base, tok, in_sems.at[half]
-        )
-        for k, ref in zip((0, 2, 1, 3), refs[8 + 4 * half : 12 + 4 * half]):
-            rows = pl.ds(base + k * tok, tok)
+            shift_ref[0], pairs, grads, 4 * half * tok, in_sems.at[half]
+        )
+    for half in range(2):
+        for k, ref in zip((0, 2, 1, 3), refs[4:8]):
             copies.append(
-                pltpu.make_async_copy(ref, hidden.at[rows], in_sems.at[half, 4 + k])
+                pltpu.make_async_copy(
+                    ref.at[pl.ds(half * tok, tok)],
+                    hidden.at[pl.ds((4 * half + k) * tok, tok)],
+                    in_sems.at[half, 4 + k],
+                )
             )
     for copy in copies:
         copy.start()
@@ -152,7 +206,7 @@
 
 
 def outer(shift, grads, hidden, tile=128, slots=26):
-    tok, width = grads[0].shape
+    tok, width = hidden[0].shape[0] // 2, grads[0].shape[1]
     rows = hidden[0].shape[1]
     return pl.pallas_call(
         functools.partial(outer_kernel, tok, tile),
@@ -160,7 +214,7 @@
             jax.ShapeDtypeStruct((rows, width), BF16),
             jax.ShapeDtypeStruct((8, 128), F32),
         ],
-        in_specs=[SMEM] + [ANYWHERE] * 16,
+        in_specs=[SMEM] + [ANYWHERE] * 8,
         out_specs=[ANYWHERE, VMEM],
         scratch_shapes=[
             pltpu.VMEM((8 * tok, width), BF16),
@@ -171,7 +225,7 @@
         ],
         compiler_params=pltpu.CompilerParams(vmem_limit_bytes=40 << 20),
         cost_estimate=QUICK,
-    )(shift, *in_hbm(grads), *in_hbm(hidden))
+    )(shift, *in_hbm([*grads, *hidden]))
 
 
 def finish(hidden_grad, gate_vals, up_vals):
@@ -196,15 +250,15 @@
         at += p0.shape[1]
 
 
-def finished(gate_pre, up_pre, sums, after):
-    vmem = pl.BlockSpec(memory_space=pltpu.VMEM)
-    terms = [term for part in sums for term in part]
-    return pl.pallas_call(
-        functools.partial(finish_kernel, len(sums)),
+def finished(gate_pre, up_pre, parts, after):
+    terms = [term for part in parts for term in part]
+    return pl.pallas_call(
+        functools.partial(finish_kernel, len(parts)),
         out_shape=[jax.ShapeDtypeStruct(gate_pre.shape, BF16)] * 2,
-        in_specs=[vmem] * (2 + len(terms)) + [pl.BlockSpec(memory_space=pl.ANY)],
-        out_specs=[vmem, vmem],
+        in_specs=[VMEM] * (2 + len(terms)) + [ANYWHERE],
+        out_specs=[VMEM] * 2,
         compiler_params=pltpu.CompilerParams(vmem_limit_bytes=16 << 20),
+        cost_estimate=QUICK,
     )(gate_pre, up_pre, *terms, after)
 
 
@@ -217,38 +271,36 @@
     def send(x, axis, distance):
         return lax.ppermute(x, axis, xor_pairs(lax.axis_size(axis), distance))
 
-    g0 = out_grad
+    mine, theirs, g0 = hidden_halves(
+        depth.astype(jnp.int32).reshape(1), gate_pre, up_pre, out_grad
+    )
+    other = send(theirs, "depth", 1)
     g2 = send(g0, "row", 2)
-    g1 = send(g0, "row", 1)
-    g3 = send(g2, "row", 1)
-
-    mine, theirs = hidden_halves(depth.astype(jnp.int32).reshape(1), gate_pre, up_pre)
-    other = send(theirs, "depth", 1)
-
-    def gather_col(x):
-        x2 = send(x, "col", 2)
-        return x, x2, send(x, "col", 1), send(x2, "col", 1)
-
-    own_layer = gather_col(mine)
-    other_layer = gather_col(other)
-
-    q0 = send(g0, "depth", 1)
-    q2 = send(q0, "row", 2)
-    q1 = send(q0, "row", 1)
-    q3 = send(q2, "row", 1)
-
-    grads = (g0, g2, g1, g3)
+    pair, h0 = stacked(g0, g2, mine, other)
+    cores = send(pair, "row", 1)
+    h2 = send(h0, "col", 2)
+    h1 = send(h0, "col", 1)
+    other_pair = send(pair, "depth", 1)
+
     def reduced(terms):
         p0, p1, p2, p3 = terms
         r2, r3, r1 = send(p2, "col", 2), send(p3, "col", 3), send(p1, "col", 1)
         return p0, r1, r2, r3
 
-    after = (own_layer[1], q0)
-    sums = [reduced(partials(shift, grads, down_weight, 0, half, after))]
-    after = (own_layer[2], other_layer[1], other_layer[2], q2)
-    sums.append(reduced(partials(shift, grads, down_weight, half, ff - half, after)))
-    weight_grad, token = outer(shift, grads + (q0, q2, q1, q3), own_layer + other_layer)
-    gate_grad, up_grad = finished(gate_pre, up_pre, sums, token)
+    most = half // 256 * 256
+    terms = partials(shift, (pair, cores), down_weight, 0, most)
+    first = reduced(terms)
+    h2, _ = lax.optimization_barrier((h2, terms[0]))
+    other_pair, _ = lax.optimization_barrier((other_pair, terms[0]))
+    h3 = send(h2, "col", 1)
+    other_cores = send(other_pair, "row", 1)
+    other_cores, shift, _ = lax.optimization_barrier((other_cores, shift, terms[0]))
+    second = reduced(partials(shift, (pair, cores), down_weight, most, ff - most))
+    shift, *first = lax.optimization_barrier((shift, *first))
+    weight_grad, token = outer(
+        shift, (pair, cores, other_pair, other_cores), (h0, h2, h1, h3)
+    )
+    gate_grad, up_grad = finished(gate_pre, up_pre, (first, second), token)
     return weight_grad, gate_grad, up_grad
 
 

time: 100 us -> 95.4 us (0.954)
  the two profiles are of different devices: /device:TPU:18 before, /device:TPU:0 now
where the time goes in v3:
time: 95.4 us; the launch traced here: 95.2 us
  Pallas kernels  41.3 us (43%)
  waiting for transfers between devices  27.4 us (29%)
  starting transfers between devices  21.5 us (23%)
  local copies, waits for them, and re-layouts  4.21 us (4%)
    ppermute x14, waiting for transfers between devices, send(): return lax.ppermute(x, axis, xor_pairs(lax.axis_size(axis), distance))  27.4 us
    pallas_call x2, Pallas kernels, partials(): pl.pallas_call(functools.partial(partial_kernel, tok, first, tiles), out_...  24.5 us
    ppermute x14, starting transfers between devices, send(): return lax.ppermute(x, axis, xor_pairs(lax.axis_size(axis), distance))  21.5 us
    pallas_call x1, Pallas kernels, outer(): pl.pallas_call(functools.partial(outer_kernel, tok, tile), out_shape=[jax...  11.8 us
    unnamed x28, local copies, waits for them, and re-layouts  4.21 us
    pallas_call x1, Pallas kernels, stacked(): pl.pallas_call(stack_kernel, out_shape=[jax.ShapeDtypeStruct((2 * tok, g0...  2.12 us
  transfers between devices with their start and end apart: 14, of which 5 were waited for; matrix products, arithmetic and copies ran while one was open for 0% of the time, Pallas kernels for 38%

profile of v3, /device:TPU:0, one launch (start us, length us, event | category | flops | bytes accessed | tf_op | source)
XLA Modules:
  0.0 95.2 jit_solution(10837055982947769629)
XLA Ops:
  0.6 1.4 %shard_map.67 = (bf16[32,3328]{1,0:T(8,128)(2,1)S(1)}, bf16[32,3328]{1,0:T(8,128)(2,1)S(1)}, bf16[32,4096]{1,0:T(8,128)(2,1)S(1)}) custom-call(s32[1]{0:T(128)} %bitcast.depth_ref, bf16[32,6656]{1,0:T(8,128)(2,1)} %gate_ref.3, bf16[32,6656]{1,0:T(8,128)(2,1)} %up_ref.3, bf16[32,4096]{1,0:T(8,128)(2,1)} %og_ref.1), custom_call_target="tpu_custom_call" | custom-call | flops 1 | bytes 1 | tf_op jit(solution)/shard_map/pallas_call | solution.py:68
  2.0 0.7 copy-done.5
  2.7 3.0 %collective-permute-start = (bf16[32,4096]{1,0:T(8,128)(2,1)S(1)}, bf16[32,4096]{1,0:T(8,128)(2,1)S(1)}, u32[]{:S(2)}, u32[]{:S(2)}) collective-permute-start(bf16[32,4096]{1,0:T(8,128)(2,1)S(1)} %get-tuple-element.29.refs_0_), channel_id=1, source_target_pairs={{0,16},{8,24},{16,0},{24,8},{1,17},{9,25},{17,1},{25,9},{2,18},{10... | collective-permute-start | bytes 786440 | tf_op jit(solution)/shard_map/ppermute | solution.py:272
  5.7 1.5 %collective-permute-start.1 = (bf16[32,3328]{1,0:T(8,128)(2,1)S(1)}, bf16[32,3328]{1,0:T(8,128)(2,1)S(1)}, u32[]{:S(2)}, u32[]{:S(2)}) collective-permute-start(bf16[32,3328]{1,0:T(8,128)(2,1)S(1)} %get-tuple-element.31), channel_id=1, source_target_pairs={{0,1},{1,0},{2,3},{3,2},{4,5},{5,4},{6,7},{7,6},{8,9},{9,8},{10,11... | collective-permute-start | bytes 638984 | tf_op jit(solution)/shard_map/ppermute | solution.py:272
  7.2 5.2 %collective-permute-done.1.refs_3_ = bf16[32,3328]{1,0:T(8,128)(2,1)S(1)} collective-permute-done((bf16[32,3328]{1,0:T(8,128)(2,1)S(1)}, bf16[32,3328]{1,0:T(8,128)(2,1)S(1)}, u32[]{:S(2)}, u32[]{:S(2)}) %collective-permute-start.1) | collective-permute-done | bytes 213024 | tf_op jit(solution)/shard_map/ppermute | solution.py:272
  12.4 0.0 collective-permute-done.refs_1_
  12.4 0.7 copy-done.13
  13.1 0.1 copy-done.12
  13.2 2.1 %shard_map.68 = (bf16[64,4096]{1,0:T(8,128)(2,1)}, bf16[64,3328]{1,0:T(8,128)(2,1)}) custom-call(bf16[32,4096]{1,0:T(8,128)(2,1)} %copy-done.4, bf16[32,4096]{1,0:T(8,128)(2,1)} %copy-done.12, bf16[32,3328]{1,0:T(8,128)(2,1)} %copy-done.5, bf16[32,3328]{1,0:T(8,128)(2,1)} %copy-done.13), custom_call_target="tpu_custom_call" | custom-call | flops 1 | bytes 1 | tf_op jit(solution)/shard_map/pallas_call | solution.py:104
  15.3 0.1 collective-permute-start.3
  15.4 1.6 %collective-permute-start.2 = (bf16[64,4096]{1,0:T(8,128)(2,1)}, bf16[64,4096]{1,0:T(8,128)(2,1)S(1)}, u32[]{:S(2)}, u32[]{:S(2)}) collective-permute-start(bf16[64,4096]{1,0:T(8,128)(2,1)} %get-tuple-element.32.pair.refs_0_), channel_id=1, source_target_pairs={{0,1},{1,0},{2,3},{3,2},{4,5},{5,4},{6,7},{7,6},{8,9},{9,8},{10,11... | collective-permute-start | bytes 1572872 | tf_op jit(solution)/shard_map/ppermute | solution.py:272
  17.0 0.6 collective-permute-done.3.cores.refs_1_
  17.5 1.2 %copy-done = bf16[64,4096]{1,0:T(8,128)(2,1)S(1)} copy-done((bf16[64,4096]{1,0:T(8,128)(2,1)S(1)}, bf16[64,4096]{1,0:T(8,128)(2,1)}, u32[]{:S(2)}) %copy-start) | copy-done | bytes 524312
  18.7 12.2 %shard_map.69 = (f32[32,3328]{1,0:T(8,128)S(1)}, bf16[32,3328]{1,0:T(8,128)(2,1)S(1)}, bf16[32,3328]{1,0:T(8,128)(2,1)S(1)}, bf16[32,3328]{1,0:T(8,128)(2,1)S(1)}) custom-call(s32[1]{0:T(128)} %bitcast.1.shift_ref, bf16[64,4096]{1,0:T(8,128)(2,1)S(1)} %copy-done, bf16[64,4096]{1,0:T(8,128)(2,1)S(1)} %collective-permute-done.3.cores.refs_1_, ...), custom_call_target="tpu_custom_call" | custom-call | flops 1 | bytes 27262976 | tf_op jit(solution)/shard_map/pallas_call | solution.py:147
  31.0 0.2 collective-permute-start.4
  31.2 2.6 %collective-permute-start.8 = (bf16[64,3328]{1,0:T(8,128)(2,1)S(1)}, bf16[64,3328]{1,0:T(8,128)(2,1)S(1)}, u32[]{:S(2)}, u32[]{:S(2)}) collective-permute-start(bf16[64,3328]{1,0:T(8,128)(2,1)S(1)} %copy-done.8), channel_id=1, source_target_pairs={{0,4},{2,6},{4,0},{6,2},{1,5},{3,7},{5,1},{7,3},{8,12},{10,14},{12... | collective-permute-start | bytes 1277960 | tf_op jit(solution)/shard_map/ppermute | solution.py:272
  33.8 1.6 %collective-permute-start.9 = (bf16[64,3328]{1,0:T(8,128)(2,1)S(1)}, bf16[64,3328]{1,0:T(8,128)(2,1)S(1)}, u32[]{:S(2)}, u32[]{:S(2)}) collective-permute-start(bf16[64,3328]{1,0:T(8,128)(2,1)S(1)} %copy-done.8), channel_id=1, source_target_pairs={{0,2},{2,0},{4,6},{6,4},{1,3},{3,1},{5,7},{7,5},{8,10},{10,8},{12,... | collective-permute-start | bytes 1277960 | tf_op jit(solution)/shard_map/ppermute | solution.py:272
  35.4 0.4 collective-permute-start.5
  35.8 17.6 %collective-permute-done.8.refs_5_ = bf16[64,3328]{1,0:T(8,128)(2,1)S(1)} collective-permute-done((bf16[64,3328]{1,0:T(8,128)(2,1)S(1)}, bf16[64,3328]{1,0:T(8,128)(2,1)S(1)}, u32[]{:S(2)}, u32[]{:S(2)}) %collective-permute-start.8) | collective-permute-done | bytes 426016 | tf_op jit(solution)/shard_map/ppermute | solution.py:272
  53.4 0.6 collective-permute-start.10
  54.1 3.4 %collective-permute-start.6 = (bf16[32,3328]{1,0:T(8,128)(2,1)S(1)}, bf16[32,3328]{1,0:T(8,128)(2,1)S(1)}, u32[]{:S(2)}, u32[]{:S(2)}) collective-permute-start(bf16[32,3328]{1,0:T(8,128)(2,1)S(1)} %get-tuple-element.37), channel_id=1, source_target_pairs={{0,4},{2,6},{4,0},{6,2},{1,5},{3,7},{5,1},{7,3},{8,12},{10,14},{12... | collective-permute-start | bytes 638984 | tf_op jit(solution)/shard_map/ppermute | solution.py:272
  57.5 0.3 collective-permute-start.7
  57.8 12.3 %shard_map.71 = (f32[32,3328]{1,0:T(8,128)S(1)}, bf16[32,3328]{1,0:T(8,128)(2,1)S(1)}, bf16[32,3328]{1,0:T(8,128)(2,1)S(1)}, bf16[32,3328]{1,0:T(8,128)(2,1)S(1)}) custom-call(s32[1]{0:T(128)} %bitcast.1.shift_ref, bf16[64,4096]{1,0:T(8,128)(2,1)S(1)} %copy-done, bf16[64,4096]{1,0:T(8,128)(2,1)S(1)} %collective-permute-done.3.cores.refs_1_, ...), custom_call_target="tpu_custom_call" | custom-call | flops 1 | bytes 27262976 | tf_op jit(solution)/shard_map/pallas_call | solution.py:147
  70.1 0.4 collective-permute-start.11
  70.5 0.9 collective-permute-done.6.refs_2_
  71.4 3.4 %collective-permute-start.12 = (bf16[32,3328]{1,0:T(8,128)(2,1)S(1)}, bf16[32,3328]{1,0:T(8,128)(2,1)S(1)}, u32[]{:S(2)}, u32[]{:S(2)}) collective-permute-start(bf16[32,3328]{1,0:T(8,128)(2,1)S(1)} %get-tuple-element.50), channel_id=1, source_target_pairs={{0,4},{2,6},{4,0},{6,2},{1,5},{3,7},{5,1},{7,3},{8,12},{10,14},{12... | collective-permute-start | bytes 638984 | tf_op jit(solution)/shard_map/ppermute | solution.py:272
  74.7 3.1 %collective-permute-done.7.refs_3_ = bf16[32,3328]{1,0:T(8,128)(2,1)S(1)} collective-permute-done((bf16[32,3328]{1,0:T(8,128)(2,1)S(1)}, bf16[32,3328]{1,0:T(8,128)(2,1)S(1)}, u32[]{:S(2)}, u32[]{:S(2)}) %collective-permute-start.7) | collective-permute-done | bytes 213024 | tf_op jit(solution)/shard_map/ppermute | solution.py:272
  77.9 2.5 %collective-permute-start.13 = (bf16[32,3328]{1,0:T(8,128)(2,1)S(1)}, bf16[32,3328]{1,0:T(8,128)(2,1)S(1)}, u32[]{:S(2)}, u32[]{:S(2)}) collective-permute-start(bf16[32,3328]{1,0:T(8,128)(2,1)S(1)} %get-tuple-element.51), channel_id=1, source_target_pairs={{0,6},{2,4},{4,2},{6,0},{1,7},{3,5},{5,3},{7,1},{8,14},{10,12},{12... | collective-permute-start | bytes 638984 | tf_op jit(solution)/shard_map/ppermute | solution.py:272
  80.4 0.7 copy-done.10
  81.1 0.8 copy-done.11
  81.9 11.8 %shard_map.70 = (bf16[3328,4096]{1,0:T(8,128)(2,1)}, f32[8,128]{1,0:T(8,128)S(1)}) custom-call(s32[1]{0:T(128)} %bitcast.1.shift_ref, bf16[64,4096]{1,0:T(8,128)(2,1)} %get-tuple-element.32.pair.refs_0_, bf16[64,4096]{1,0:T(8,128)(2,1)} %copy-done.1, bf16[64,4096]{1,0:T(8,128)(2,1)} %copy-done.6, bf16[64,4096]{1,0:T(8,128)(2,1)} %copy-done.7, ...), custom_call_target="tpu_custom_call" | custom-call | flops 1 | bytes 1 | tf_op jit(solution)/shard_map/pallas_call | solution.py:211
  93.8 1.4 %shard_map.72 = (bf16[32,6656]{1,0:T(8,128)(2,1)}, bf16[32,6656]{1,0:T(8,128)(2,1)}) custom-call(bf16[32,6656]{1,0:T(8,128)(2,1)S(1)} %copy-done.2, bf16[32,6656]{1,0:T(8,128)(2,1)S(1)} %copy-done.3, f32[32,3328]{1,0:T(8,128)S(1)} %get-tuple-element.44.refs_0_, bf16[32,3328]{1,0:T(8,128)(2,1)S(1)} %collective-permute-done.5.refs_1_, ...), custom_call_target="tpu_custom_call" | custom-call | flops 1 | bytes 1 | tf_op jit(solution)/shard_map/pallas_call | solution.py:255
  (30 shorter events, 0.1 us)
Async XLA Ops:
  2.0 0.7 copy-start.5
  2.7 9.7 %copy-start.4 = (bf16[32,4096]{1,0:T(8,128)(2,1)}, bf16[32,4096]{1,0:T(8,128)(2,1)S(1)}, u32[]{:S(2)}) copy-start(bf16[32,4096]{1,0:T(8,128)(2,1)S(1)} %get-tuple-element.29.refs_0_) | copy-start | bytes 786436
  2.7 9.7 %collective-permute-start = (bf16[32,4096]{1,0:T(8,128)(2,1)S(1)}, bf16[32,4096]{1,0:T(8,128)(2,1)S(1)}, u32[]{:S(2)}, u32[]{:S(2)}) collective-permute-start(bf16[32,4096]{1,0:T(8,128)(2,1)S(1)} %get-tuple-element.29.refs_0_), channel_id=1, source_target_pairs={{0,16},{8,24},{16,0},{24,8},{1,17},{9,25},{17,1},{25,9},{2,18},{10... | collective-permute-start | bytes 786440 | tf_op jit(solution)/shard_map/ppermute | solution.py:272
  5.7 6.7 %collective-permute-start.1 = (bf16[32,3328]{1,0:T(8,128)(2,1)S(1)}, bf16[32,3328]{1,0:T(8,128)(2,1)S(1)}, u32[]{:S(2)}, u32[]{:S(2)}) collective-permute-start(bf16[32,3328]{1,0:T(8,128)(2,1)S(1)} %get-tuple-element.31), channel_id=1, source_target_pairs={{0,1},{1,0},{2,3},{3,2},{4,5},{5,4},{6,7},{7,6},{8,9},{9,8},{10,11... | collective-permute-start | bytes 638984 | tf_op jit(solution)/shard_map/ppermute | solution.py:272
  12.4 0.7 copy-start.13
  12.4 0.8 copy-start.12
  15.3 2.2 %collective-permute-start.3 = (bf16[64,4096]{1,0:T(8,128)(2,1)}, bf16[64,4096]{1,0:T(8,128)(2,1)S(1)}, u32[]{:S(2)}, u32[]{:S(2)}) collective-permute-start(bf16[64,4096]{1,0:T(8,128)(2,1)} %get-tuple-element.32.pair.refs_0_), channel_id=1, source_target_pairs={{0,8},{8,0},{16,24},{24,16},{1,9},{9,1},{17,25},{25,17},{2,10},{10... | collective-permute-start | bytes 1572872 | tf_op jit(solution)/shard_map/ppermute | solution.py:272
  15.4 15.6 %collective-permute-start.2 = (bf16[64,4096]{1,0:T(8,128)(2,1)}, bf16[64,4096]{1,0:T(8,128)(2,1)S(1)}, u32[]{:S(2)}, u32[]{:S(2)}) collective-permute-start(bf16[64,4096]{1,0:T(8,128)(2,1)} %get-tuple-element.32.pair.refs_0_), channel_id=1, source_target_pairs={{0,1},{1,0},{2,3},{3,2},{4,5},{5,4},{6,7},{7,6},{8,9},{9,8},{10,11... | collective-permute-start | bytes 1572872 | tf_op jit(solution)/shard_map/ppermute | solution.py:272
  17.5 52.6 %copy-start.1 = (bf16[64,4096]{1,0:T(8,128)(2,1)}, bf16[64,4096]{1,0:T(8,128)(2,1)S(1)}, u32[]{:S(2)}) copy-start(bf16[64,4096]{1,0:T(8,128)(2,1)S(1)} %collective-permute-done.3.cores.refs_1_) | copy-start | bytes 1572868
  17.5 1.2 %copy-start = (bf16[64,4096]{1,0:T(8,128)(2,1)S(1)}, bf16[64,4096]{1,0:T(8,128)(2,1)}, u32[]{:S(2)}) copy-start(bf16[64,4096]{1,0:T(8,128)(2,1)} %get-tuple-element.32.pair.refs_0_) | copy-start | bytes 1572868
  18.7 12.4 %copy-start.8 = (bf16[64,3328]{1,0:T(8,128)(2,1)S(1)}, bf16[64,3328]{1,0:T(8,128)(2,1)}, u32[]{:S(2)}) copy-start(bf16[64,3328]{1,0:T(8,128)(2,1)} %get-tuple-element.41.refs_4_) | copy-start | bytes 1277956
  18.7 75.0 %copy-start.2 = (bf16[32,6656]{1,0:T(8,128)(2,1)S(1)}, bf16[32,6656]{1,0:T(8,128)(2,1)}, u32[]{:S(2)}) copy-start(bf16[32,6656]{1,0:T(8,128)(2,1)} %gate_ref.3) | copy-start | bytes 1277956
  18.7 75.0 %copy-start.3 = (bf16[32,6656]{1,0:T(8,128)(2,1)S(1)}, bf16[32,6656]{1,0:T(8,128)(2,1)}, u32[]{:S(2)}) copy-start(bf16[32,6656]{1,0:T(8,128)(2,1)} %up_ref.3) | copy-start | bytes 1277956
  31.0 49.4 %copy-start.6 = (bf16[64,4096]{1,0:T(8,128)(2,1)}, bf16[64,4096]{1,0:T(8,128)(2,1)S(1)}, u32[]{:S(2)}) copy-start(bf16[64,4096]{1,0:T(8,128)(2,1)S(1)} %collective-permute-done.2.refs_2_) | copy-start | bytes 1572868
  31.0 26.5 %collective-permute-start.4 = (bf16[64,4096]{1,0:T(8,128)(2,1)S(1)}, bf16[64,4096]{1,0:T(8,128)(2,1)S(1)}, u32[]{:S(2)}, u32[]{:S(2)}) collective-permute-start(bf16[64,4096]{1,0:T(8,128)(2,1)S(1)} %collective-permute-done.2.refs_2_), channel_id=1, source_target_pairs={{0,8},{8,0},{16,24},{24,16},{1,9},{9,1},{17,25},{25,17},{2,10},{10... | collective-permute-start | bytes 1572872 | tf_op jit(solution)/shard_map/ppermute | solution.py:272
  31.2 22.2 %collective-permute-start.8 = (bf16[64,3328]{1,0:T(8,128)(2,1)S(1)}, bf16[64,3328]{1,0:T(8,128)(2,1)S(1)}, u32[]{:S(2)}, u32[]{:S(2)}) collective-permute-start(bf16[64,3328]{1,0:T(8,128)(2,1)S(1)} %copy-done.8), channel_id=1, source_target_pairs={{0,4},{2,6},{4,0},{6,2},{1,5},{3,7},{5,1},{7,3},{8,12},{10,14},{12... | collective-permute-start | bytes 1277960 | tf_op jit(solution)/shard_map/ppermute | solution.py:272
  33.8 46.6 %collective-permute-start.9 = (bf16[64,3328]{1,0:T(8,128)(2,1)S(1)}, bf16[64,3328]{1,0:T(8,128)(2,1)S(1)}, u32[]{:S(2)}, u32[]{:S(2)}) collective-permute-start(bf16[64,3328]{1,0:T(8,128)(2,1)S(1)} %copy-done.8), channel_id=1, source_target_pairs={{0,2},{2,0},{4,6},{6,4},{1,3},{3,1},{5,7},{7,5},{8,10},{10,8},{12,... | collective-permute-start | bytes 1277960 | tf_op jit(solution)/shard_map/ppermute | solution.py:272
  35.4 34.8 %collective-permute-start.5 = (bf16[32,3328]{1,0:T(8,128)(2,1)S(1)}, bf16[32,3328]{1,0:T(8,128)(2,1)S(1)}, u32[]{:S(2)}, u32[]{:S(2)}) collective-permute-start(bf16[32,3328]{1,0:T(8,128)(2,1)S(1)} %get-tuple-element.36), channel_id=1, source_target_pairs={{0,2},{2,0},{4,6},{6,4},{1,3},{3,1},{5,7},{7,5},{8,10},{10,8},{12,... | collective-permute-start | bytes 638984 | tf_op jit(solution)/shard_map/ppermute | solution.py:272
  53.4 27.0 %copy-start.9 = (bf16[64,3328]{1,0:T(8,128)(2,1)}, bf16[64,3328]{1,0:T(8,128)(2,1)S(1)}, u32[]{:S(2)}) copy-start(bf16[64,3328]{1,0:T(8,128)(2,1)S(1)} %collective-permute-done.8.refs_5_) | copy-start | bytes 1277956
  53.4 26.9 %collective-permute-start.10 = (bf16[64,3328]{1,0:T(8,128)(2,1)S(1)}, bf16[64,3328]{1,0:T(8,128)(2,1)S(1)}, u32[]{:S(2)}, u32[]{:S(2)}) collective-permute-start(bf16[64,3328]{1,0:T(8,128)(2,1)S(1)} %collective-permute-done.8.refs_5_), channel_id=1, source_target_pairs={{0,2},{2,0},{4,6},{6,4},{1,3},{3,1},{5,7},{7,5},{8,10},{10,8},{12,... | collective-permute-start | bytes 1277960 | tf_op jit(solution)/shard_map/ppermute | solution.py:272
  54.1 17.3 %collective-permute-start.6 = (bf16[32,3328]{1,0:T(8,128)(2,1)S(1)}, bf16[32,3328]{1,0:T(8,128)(2,1)S(1)}, u32[]{:S(2)}, u32[]{:S(2)}) collective-permute-start(bf16[32,3328]{1,0:T(8,128)(2,1)S(1)} %get-tuple-element.37), channel_id=1, source_target_pairs={{0,4},{2,6},{4,0},{6,2},{1,5},{3,7},{5,1},{7,3},{8,12},{10,14},{12... | collective-permute-start | bytes 638984 | tf_op jit(solution)/shard_map/ppermute | solution.py:272
  57.5 22.9 %copy-start.7 = (bf16[64,4096]{1,0:T(8,128)(2,1)}, bf16[64,4096]{1,0:T(8,128)(2,1)S(1)}, u32[]{:S(2)}) copy-start(bf16[64,4096]{1,0:T(8,128)(2,1)S(1)} %collective-permute-done.4.refs_3_) | copy-start | bytes 1572868
  57.5 20.4 %collective-permute-start.7 = (bf16[32,3328]{1,0:T(8,128)(2,1)S(1)}, bf16[32,3328]{1,0:T(8,128)(2,1)S(1)}, u32[]{:S(2)}, u32[]{:S(2)}) collective-permute-start(bf16[32,3328]{1,0:T(8,128)(2,1)S(1)} %get-tuple-element.38), channel_id=1, source_target_pairs={{0,6},{2,4},{4,2},{6,0},{1,7},{3,5},{5,3},{7,1},{8,14},{10,12},{12... | collective-permute-start | bytes 638984 | tf_op jit(solution)/shard_map/ppermute | solution.py:272
  70.1 23.6 %collective-permute-start.11 = (bf16[32,3328]{1,0:T(8,128)(2,1)S(1)}, bf16[32,3328]{1,0:T(8,128)(2,1)S(1)}, u32[]{:S(2)}, u32[]{:S(2)}) collective-permute-start(bf16[32,3328]{1,0:T(8,128)(2,1)S(1)} %get-tuple-element.49), channel_id=1, source_target_pairs={{0,2},{2,0},{4,6},{6,4},{1,3},{3,1},{5,7},{7,5},{8,10},{10,8},{12,... | collective-permute-start | bytes 638984 | tf_op jit(solution)/shard_map/ppermute | solution.py:272
  71.4 22.4 %collective-permute-start.12 = (bf16[32,3328]{1,0:T(8,128)(2,1)S(1)}, bf16[32,3328]{1,0:T(8,128)(2,1)S(1)}, u32[]{:S(2)}, u32[]{:S(2)}) collective-permute-start(bf16[32,3328]{1,0:T(8,128)(2,1)S(1)} %get-tuple-element.50), channel_id=1, source_target_pairs={{0,4},{2,6},{4,0},{6,2},{1,5},{3,7},{5,1},{7,3},{8,12},{10,14},{12... | collective-permute-start | bytes 638984 | tf_op jit(solution)/shard_map/ppermute | solution.py:272
  77.9 15.9 %collective-permute-start.13 = (bf16[32,3328]{1,0:T(8,128)(2,1)S(1)}, bf16[32,3328]{1,0:T(8,128)(2,1)S(1)}, u32[]{:S(2)}, u32[]{:S(2)}) collective-permute-start(bf16[32,3328]{1,0:T(8,128)(2,1)S(1)} %get-tuple-element.51), channel_id=1, source_target_pairs={{0,6},{2,4},{4,2},{6,0},{1,7},{3,5},{5,3},{7,1},{8,14},{10,12},{12... | collective-permute-start | bytes 638984 | tf_op jit(solution)/shard_map/ppermute | solution.py:272
  80.4 0.8 copy-start.10
  81.1 0.8 copy-start.11

commit v4 on v2

--- a/solution.py
+++ b/solution.py
@@ -73,11 +73,11 @@
         )
         for i, (at, size) in enumerate(tiles)
     ]
-    for copy in copies:
+    for copy in copies + fetches[:1]:
         copy.start()
     for copy in copies:
         copy.wait()
-    for fetch in fetches:
+    for fetch in fetches[1:]:
         fetch.start()
     for fetch, (at, size) in zip(fetches, tiles):
         fetch.wait()
@@ -108,7 +108,7 @@
         ],
         compiler_params=pltpu.CompilerParams(vmem_limit_bytes=40 << 20),
         cost_estimate=QUICK,
-    )(shift, *in_hbm([*grads, weight, *after]))
+    )(shift, *grads, *in_hbm([weight, *after]))
 
 
 def outer_kernel(tok, tile, shift_ref, *refs):

time: 84.8 us -> 82.9 us (0.978)
  Pallas kernels: 40.8 us -> 38.5 us
  starting transfers between devices: 24.5 us -> 23.3 us
  waiting for transfers between devices: 14.2 us -> 15.3 us
    pallas_call x2, Pallas kernels: 26.8 us -> 24.5 us  [partials(): pl.pallas_call(functools.partial(partial_kernel, tok, first, tiles, len(a...]
    ppermute x20, starting transfers between devices: 24.5 us -> 23.3 us  [send(): return lax.ppermute(x, axis, xor_pairs(lax.axis_size(axis), distance))]
    ppermute x20, waiting for transfers between devices: 14.2 us -> 15.3 us  [send(): return lax.ppermute(x, axis, xor_pairs(lax.axis_size(axis), distance))]
    unnamed x42 -> x44, local copies, waits for them, and re-layouts: 4.26 us -> 4.61 us
  transfers between devices with their start and end apart: 20 -> 20, of which waited for: 4 -> 5; matrix products, arithmetic and copies ran while one was open for 0% -> 0% of each run, Pallas kernels for 47% -> 45%
where the time goes in v4:
time: 82.9 us; the launch traced here: 82.6 us
  Pallas kernels  38.5 us (46%)
  starting transfers between devices  23.3 us (28%)
  waiting for transfers between devices  15.3 us (18%)
  local copies, waits for them, and re-layouts  4.61 us (6%)
  between operations  0.87 us (1%)
    pallas_call x2, Pallas kernels, partials(): pl.pallas_call(functools.partial(partial_kernel, tok, first, tiles, len(a...  24.5 us
    ppermute x20, starting transfers between devices, send(): return lax.ppermute(x, axis, xor_pairs(lax.axis_size(axis), distance))  23.3 us
    ppermute x20, waiting for transfers between devices, send(): return lax.ppermute(x, axis, xor_pairs(lax.axis_size(axis), distance))  15.3 us
    pallas_call x1, Pallas kernels, outer(): pl.pallas_call(functools.partial(outer_kernel, tok, tile), out_shape=[jax...  11.8 us
    unnamed x44, local copies, waits for them, and re-layouts  4.61 us
    pallas_call x2, Pallas kernels, finished(): pl.pallas_call(finish_kernel, grid=(1,), out_shape=[jax.ShapeDtypeStruct(...  1.98 us
  transfers between devices with their start and end apart: 20, of which 5 were waited for; matrix products, arithmetic and copies ran while one was open for 0% of the time, Pallas kernels for 45%

profile of v4, /device:TPU:0, one launch (start us, length us, event | category | flops | bytes accessed | tf_op | source)
XLA Modules:
  0.0 82.6 jit_solution(14740072372991829364)
XLA Ops:
  0.6 3.0 %collective-permute-start = (bf16[32,4096]{1,0:T(8,128)(2,1)}, bf16[32,4096]{1,0:T(8,128)(2,1)S(1)}, u32[]{:S(2)}, u32[]{:S(2)}) collective-permute-start(bf16[32,4096]{1,0:T(8,128)(2,1)} %refs_0_.5), channel_id=1, source_target_pairs={{0,16},{8,24},{16,0},{24,8},{1,17},{9,25},{17,1},{25,9},{2,18},{10... | collective-permute-start | bytes 786440 | tf_op jit(solution)/shard_map/ppermute | solution.py:219
  3.7 1.0 %copy-done = bf16[32,6656]{1,0:T(8,128)(2,1)S(1)} copy-done((bf16[32,6656]{1,0:T(8,128)(2,1)S(1)}, bf16[32,6656]{1,0:T(8,128)(2,1)}, u32[]{:S(2)}) %copy-start) | copy-done | bytes 426008
  4.7 1.0 %copy-done.2 = bf16[32,6656]{1,0:T(8,128)(2,1)S(1)} copy-done((bf16[32,6656]{1,0:T(8,128)(2,1)S(1)}, bf16[32,6656]{1,0:T(8,128)(2,1)}, u32[]{:S(2)}) %copy-start.2) | copy-done | bytes 426008
  5.7 0.2 shard_map.67
  5.9 1.6 %collective-permute-start.10 = (bf16[32,3328]{1,0:T(8,128)(2,1)S(1)}, bf16[32,3328]{1,0:T(8,128)(2,1)S(1)}, u32[]{:S(2)}, u32[]{:S(2)}) collective-permute-start(bf16[32,3328]{1,0:T(8,128)(2,1)S(1)} %get-tuple-element.21), channel_id=1, source_target_pairs={{0,1},{1,0},{2,3},{3,2},{4,5},{5,4},{6,7},{7,6},{8,9},{9,8},{10,11... | collective-permute-start | bytes 638984 | tf_op jit(solution)/shard_map/ppermute | solution.py:219
  7.4 2.6 %collective-permute-start.7 = (bf16[32,3328]{1,0:T(8,128)(2,1)S(1)}, bf16[32,3328]{1,0:T(8,128)(2,1)S(1)}, u32[]{:S(2)}, u32[]{:S(2)}) collective-permute-start(bf16[32,3328]{1,0:T(8,128)(2,1)S(1)} %get-tuple-element.20.refs_8_), channel_id=1, source_target_pairs={{0,4},{2,6},{4,0},{6,2},{1,5},{3,7},{5,1},{7,3},{8,12},{10,14},{12... | collective-permute-start | bytes 638984 | tf_op jit(solution)/shard_map/ppermute | solution.py:219
  10.0 1.6 %collective-permute-start.8 = (bf16[32,3328]{1,0:T(8,128)(2,1)S(1)}, bf16[32,3328]{1,0:T(8,128)(2,1)S(1)}, u32[]{:S(2)}, u32[]{:S(2)}) collective-permute-start(bf16[32,3328]{1,0:T(8,128)(2,1)S(1)} %get-tuple-element.20.refs_8_), channel_id=1, source_target_pairs={{0,2},{2,0},{4,6},{6,4},{1,3},{3,1},{5,7},{7,5},{8,10},{10,8},{12,... | collective-permute-start | bytes 638984 | tf_op jit(solution)/shard_map/ppermute | solution.py:219
  11.6 1.1 %collective-permute-done.10.refs_5_.refs_12_ = bf16[32,3328]{1,0:T(8,128)(2,1)S(1)} collective-permute-done((bf16[32,3328]{1,0:T(8,128)(2,1)S(1)}, bf16[32,3328]{1,0:T(8,128)(2,1)S(1)}, u32[]{:S(2)}, u32[]{:S(2)}) %collective-permute-start.10) | collective-permute-done | bytes 213024 | tf_op jit(solution)/shard_map/ppermute | solution.py:219
  12.7 1.5 %collective-permute-start.3 = (bf16[32,4096]{1,0:T(8,128)(2,1)}, bf16[32,4096]{1,0:T(8,128)(2,1)S(1)}, u32[]{:S(2)}, u32[]{:S(2)}) collective-permute-start(bf16[32,4096]{1,0:T(8,128)(2,1)} %refs_0_.5), channel_id=1, source_target_pairs={{0,1},{1,0},{2,3},{3,2},{4,5},{5,4},{6,7},{7,6},{8,9},{9,8},{10,11... | collective-permute-start | bytes 786440 | tf_op jit(solution)/shard_map/ppermute | solution.py:219
  14.2 6.5 %collective-permute-done.7.refs_9_.refs_6_ = bf16[32,3328]{1,0:T(8,128)(2,1)S(1)} collective-permute-done((bf16[32,3328]{1,0:T(8,128)(2,1)S(1)}, bf16[32,3328]{1,0:T(8,128)(2,1)S(1)}, u32[]{:S(2)}, u32[]{:S(2)}) %collective-permute-start.7) | collective-permute-done | bytes 213024 | tf_op jit(solution)/shard_map/ppermute | solution.py:219
  20.7 0.2 collective-permute-done.8.refs_10_.refs_7_
  20.9 3.8 %collective-permute-start.12 = (bf16[32,3328]{1,0:T(8,128)(2,1)S(1)}, bf16[32,3328]{1,0:T(8,128)(2,1)S(1)}, u32[]{:S(2)}, u32[]{:S(2)}) collective-permute-start(bf16[32,3328]{1,0:T(8,128)(2,1)S(1)} %collective-permute-done.10.refs_5_.refs_12_), channel_id=1, source_target_pairs={{0,2},{2,0},{4,6},{6,4},{1,3},{3,1},{5,7},{7,5},{8,10},{10,8},{12,... | collective-permute-start | bytes 638984 | tf_op jit(solution)/shard_map/ppermute | solution.py:219
  24.6 0.1 collective-permute-start.9
  24.7 0.5 collective-permute-start.4
  25.3 0.0 copy-start.4
  25.3 1.0 %copy-done.4 = bf16[32,4096]{1,0:T(8,128)(2,1)S(1)} copy-done((bf16[32,4096]{1,0:T(8,128)(2,1)S(1)}, bf16[32,4096]{1,0:T(8,128)(2,1)}, u32[]{:S(2)}) %copy-start.4) | copy-done | bytes 262168
  26.3 12.2 %shard_map.68 = (f32[32,3328]{1,0:T(8,128)S(1)}, bf16[32,3328]{1,0:T(8,128)(2,1)S(1)}, bf16[32,3328]{1,0:T(8,128)(2,1)S(1)}, bf16[32,3328]{1,0:T(8,128)(2,1)S(1)}) custom-call(s32[1]{0:T(128)} %bitcast.shift_ref, bf16[32,4096]{1,0:T(8,128)(2,1)S(1)} %copy-done.4, bf16[32,4096]{1,0:T(8,128)(2,1)S(1)} %collective-permute-done.refs_1_, ...), custom_call_target="tpu_custom_call" | custom-call | flops 1 | bytes 1 | tf_op jit(solution)/shard_map/pallas_call | solution.py:97
  38.5 0.7 copy-done.8
  39.3 1.9 %collective-permute-start.14 = (bf16[32,3328]{1,0:T(8,128)(2,1)S(1)}, bf16[32,3328]{1,0:T(8,128)(2,1)S(1)}, u32[]{:S(2)}, u32[]{:S(2)}) collective-permute-start(bf16[32,3328]{1,0:T(8,128)(2,1)S(1)} %get-tuple-element.23), channel_id=1, source_target_pairs={{0,2},{2,0},{4,6},{6,4},{1,3},{3,1},{5,7},{7,5},{8,10},{10,8},{12,... | collective-permute-start | bytes 638984 | tf_op jit(solution)/shard_map/ppermute | solution.py:219
  41.2 0.1 collective-permute-start.15
  41.3 2.4 %collective-permute-start.16 = (bf16[32,3328]{1,0:T(8,128)(2,1)S(1)}, bf16[32,3328]{1,0:T(8,128)(2,1)S(1)}, u32[]{:S(2)}, u32[]{:S(2)}) collective-permute-start(bf16[32,3328]{1,0:T(8,128)(2,1)S(1)} %get-tuple-element.25), channel_id=1, source_target_pairs={{0,6},{2,4},{4,2},{6,0},{1,7},{3,5},{5,3},{7,1},{8,14},{10,12},{12... | collective-permute-start | bytes 638984 | tf_op jit(solution)/shard_map/ppermute | solution.py:219
  43.7 12.3 %shard_map.71 = (f32[32,3328]{1,0:T(8,128)S(1)}, bf16[32,3328]{1,0:T(8,128)(2,1)S(1)}, bf16[32,3328]{1,0:T(8,128)(2,1)S(1)}, bf16[32,3328]{1,0:T(8,128)(2,1)S(1)}) custom-call(s32[1]{0:T(128)} %bitcast.shift_ref, bf16[32,4096]{1,0:T(8,128)(2,1)S(1)} %copy-done.4, bf16[32,4096]{1,0:T(8,128)(2,1)S(1)} %collective-permute-done.refs_1_, ...), custom_call_target="tpu_custom_call" | custom-call | flops 1 | bytes 1 | tf_op jit(solution)/shard_map/pallas_call | solution.py:97
  56.1 1.1 %collective-permute-start.13 = (bf16[32,3328]{1,0:T(8,128)(2,1)}, bf16[32,3328]{1,0:T(8,128)(2,1)S(1)}, u32[]{:S(2)}, u32[]{:S(2)}) collective-permute-start(bf16[32,3328]{1,0:T(8,128)(2,1)} %copy-done.15), channel_id=1, source_target_pairs={{0,2},{2,0},{4,6},{6,4},{1,3},{3,1},{5,7},{7,5},{8,10},{10,8},{12,... | collective-permute-start | bytes 638984 | tf_op jit(solution)/shard_map/ppermute | solution.py:219
  57.2 1.0 %collective-permute-start.17 = (bf16[32,3328]{1,0:T(8,128)(2,1)S(1)}, bf16[32,3328]{1,0:T(8,128)(2,1)S(1)}, u32[]{:S(2)}, u32[]{:S(2)}) collective-permute-start(bf16[32,3328]{1,0:T(8,128)(2,1)S(1)} %get-tuple-element.29), channel_id=1, source_target_pairs={{0,2},{2,0},{4,6},{6,4},{1,3},{3,1},{5,7},{7,5},{8,10},{10,8},{12,... | collective-permute-start | bytes 638984 | tf_op jit(solution)/shard_map/ppermute | solution.py:219
  58.2 1.2 %collective-permute-done.15.r2 = bf16[32,3328]{1,0:T(8,128)(2,1)S(1)} collective-permute-done((bf16[32,3328]{1,0:T(8,128)(2,1)S(1)}, bf16[32,3328]{1,0:T(8,128)(2,1)S(1)}, u32[]{:S(2)}, u32[]{:S(2)}) %collective-permute-start.15) | collective-permute-done | bytes 213024 | tf_op jit(solution)/shard_map/ppermute | solution.py:219
  59.4 2.2 %collective-permute-start.19 = (bf16[32,3328]{1,0:T(8,128)(2,1)S(1)}, bf16[32,3328]{1,0:T(8,128)(2,1)S(1)}, u32[]{:S(2)}, u32[]{:S(2)}) collective-permute-start(bf16[32,3328]{1,0:T(8,128)(2,1)S(1)} %get-tuple-element.31), channel_id=1, source_target_pairs={{0,6},{2,4},{4,2},{6,0},{1,7},{3,5},{5,3},{7,1},{8,14},{10,12},{12... | collective-permute-start | bytes 638984 | tf_op jit(solution)/shard_map/ppermute | solution.py:219
  61.6 1.0 %shard_map.69 = (bf16[32,6656]{1,0:T(8,128)(2,1)}, bf16[32,6656]{1,0:T(8,128)(2,1)}, f32[8,128]{1,0:T(8,128)S(1)}) custom-call(bf16[32,6656]{1,0:T(8,128)(2,1)S(1)} %copy-done.1, bf16[32,6656]{1,0:T(8,128)(2,1)S(1)} %copy-done.3, f32[32,3328]{1,0:T(8,128)S(1)} %copy-done.9, bf16[32,3328]{1,0:T(8,128)(2,1)S(1)} %collective-permute-done.14.r1, ...), custom_call_target="tpu_custom_call" | custom-call | flops 1 | bytes 1 | tf_op jit(solution)/shard_map/pallas_call | solution.py:199
  62.6 6.4 %collective-permute-done.13.refs_15_ = bf16[32,3328]{1,0:T(8,128)(2,1)S(1)} collective-permute-done((bf16[32,3328]{1,0:T(8,128)(2,1)}, bf16[32,3328]{1,0:T(8,128)(2,1)S(1)}, u32[]{:S(2)}, u32[]{:S(2)}) %collective-permute-start.13) | collective-permute-done | bytes 213024 | tf_op jit(solution)/shard_map/ppermute | solution.py:219
  69.0 0.6 copy-done.21
  69.7 0.1 copy-done.19
  69.8 11.8 %shard_map.70 = (bf16[3328,4096]{1,0:T(8,128)(2,1)}, f32[8,128]{1,0:T(8,128)S(1)}) custom-call(s32[1]{0:T(128)} %bitcast.shift_ref, bf16[32,4096]{1,0:T(8,128)(2,1)} %refs_0_.5, bf16[32,4096]{1,0:T(8,128)(2,1)} %copy-done.5, bf16[32,4096]{1,0:T(8,128)(2,1)} %copy-done.6, bf16[32,4096]{1,0:T(8,128)(2,1)} %copy-done.7, bf16[32,4096]{1,0:T(8,128)(2,1)} %copy-done.11, ...), custom_call_target="tpu_custom_call" | custom-call | flops 1 | bytes 1 | tf_op jit(solution)/shard_map/pallas_call | solution.py:157
  81.6 1.0 %shard_map.72 = (bf16[32,6656]{1,0:T(8,128)(2,1)}, bf16[32,6656]{1,0:T(8,128)(2,1)}, f32[8,128]{1,0:T(8,128)}) custom-call(bf16[32,6656]{1,0:T(8,128)(2,1)S(1)} %copy-done.1, bf16[32,6656]{1,0:T(8,128)(2,1)S(1)} %copy-done.3, f32[32,3328]{1,0:T(8,128)S(1)} %get-tuple-element.28.p0, ...), custom_call_target="tpu_custom_call", output_to_operand_aliasing={{0}: (6, {}), {1}: (7, {})} | custom-call | flops 1 | bytes 1 | tf_op jit(solution)/shard_map/pallas_call | solution.py:199
  (58 shorter events, 0.1 us)
Async XLA Ops:
  0.6 13.5 %collective-permute-start = (bf16[32,4096]{1,0:T(8,128)(2,1)}, bf16[32,4096]{1,0:T(8,128)(2,1)S(1)}, u32[]{:S(2)}, u32[]{:S(2)}) collective-permute-start(bf16[32,4096]{1,0:T(8,128)(2,1)} %refs_0_.5), channel_id=1, source_target_pairs={{0,16},{8,24},{16,0},{24,8},{1,17},{9,25},{17,1},{25,9},{2,18},{10... | collective-permute-start | bytes 786440 | tf_op jit(solution)/shard_map/ppermute | solution.py:219
  5.9 50.2 %copy-start.10 = (bf16[32,3328]{1,0:T(8,128)(2,1)}, bf16[32,3328]{1,0:T(8,128)(2,1)S(1)}, u32[]{:S(2)}) copy-start(bf16[32,3328]{1,0:T(8,128)(2,1)S(1)} %get-tuple-element.20.refs_8_) | copy-start | bytes 638980
  5.9 6.8 %collective-permute-start.10 = (bf16[32,3328]{1,0:T(8,128)(2,1)S(1)}, bf16[32,3328]{1,0:T(8,128)(2,1)S(1)}, u32[]{:S(2)}, u32[]{:S(2)}) collective-permute-start(bf16[32,3328]{1,0:T(8,128)(2,1)S(1)} %get-tuple-element.21), channel_id=1, source_target_pairs={{0,1},{1,0},{2,3},{3,2},{4,5},{5,4},{6,7},{7,6},{8,9},{9,8},{10,11... | collective-permute-start | bytes 638984 | tf_op jit(solution)/shard_map/ppermute | solution.py:219
  7.4 17.2 %collective-permute-start.1 = (bf16[32,4096]{1,0:T(8,128)(2,1)}, bf16[32,4096]{1,0:T(8,128)(2,1)S(1)}, u32[]{:S(2)}, u32[]{:S(2)}) collective-permute-start(bf16[32,4096]{1,0:T(8,128)(2,1)} %refs_0_.5), channel_id=1, source_target_pairs={{0,8},{8,0},{16,24},{24,16},{1,9},{9,1},{17,25},{25,17},{2,10},{10... | collective-permute-start | bytes 786440 | tf_op jit(solution)/shard_map/ppermute | solution.py:219
  7.4 13.2 %collective-permute-start.7 = (bf16[32,3328]{1,0:T(8,128)(2,1)S(1)}, bf16[32,3328]{1,0:T(8,128)(2,1)S(1)}, u32[]{:S(2)}, u32[]{:S(2)}) collective-permute-start(bf16[32,3328]{1,0:T(8,128)(2,1)S(1)} %get-tuple-element.20.refs_8_), channel_id=1, source_target_pairs={{0,4},{2,6},{4,0},{6,2},{1,5},{3,7},{5,1},{7,3},{8,12},{10,14},{12... | collective-permute-start | bytes 638984 | tf_op jit(solution)/shard_map/ppermute | solution.py:219
  10.0 10.8 %collective-permute-start.8 = (bf16[32,3328]{1,0:T(8,128)(2,1)S(1)}, bf16[32,3328]{1,0:T(8,128)(2,1)S(1)}, u32[]{:S(2)}, u32[]{:S(2)}) collective-permute-start(bf16[32,3328]{1,0:T(8,128)(2,1)S(1)} %get-tuple-element.20.refs_8_), channel_id=1, source_target_pairs={{0,2},{2,0},{4,6},{6,4},{1,3},{3,1},{5,7},{7,5},{8,10},{10,8},{12,... | collective-permute-start | bytes 638984 | tf_op jit(solution)/shard_map/ppermute | solution.py:219
  12.7 12.1 %collective-permute-start.3 = (bf16[32,4096]{1,0:T(8,128)(2,1)}, bf16[32,4096]{1,0:T(8,128)(2,1)S(1)}, u32[]{:S(2)}, u32[]{:S(2)}) collective-permute-start(bf16[32,4096]{1,0:T(8,128)(2,1)} %refs_0_.5), channel_id=1, source_target_pairs={{0,1},{1,0},{2,3},{3,2},{4,5},{5,4},{6,7},{7,6},{8,9},{9,8},{10,11... | collective-permute-start | bytes 786440 | tf_op jit(solution)/shard_map/ppermute | solution.py:219
  14.2 41.9 %copy-start.5 = (bf16[32,4096]{1,0:T(8,128)(2,1)}, bf16[32,4096]{1,0:T(8,128)(2,1)S(1)}, u32[]{:S(2)}) copy-start(bf16[32,4096]{1,0:T(8,128)(2,1)S(1)} %collective-permute-done.refs_1_) | copy-start | bytes 786436
  14.2 11.1 %collective-permute-start.2 = (bf16[32,4096]{1,0:T(8,128)(2,1)S(1)}, bf16[32,4096]{1,0:T(8,128)(2,1)S(1)}, u32[]{:S(2)}, u32[]{:S(2)}) collective-permute-start(bf16[32,4096]{1,0:T(8,128)(2,1)S(1)} %collective-permute-done.refs_1_), channel_id=1, source_target_pairs={{0,8},{8,0},{16,24},{24,16},{1,9},{9,1},{17,25},{25,17},{2,10},{10... | collective-permute-start | bytes 786440 | tf_op jit(solution)/shard_map/ppermute | solution.py:219
  20.7 23.0 %copy-start.13 = (bf16[32,3328]{1,0:T(8,128)(2,1)}, bf16[32,3328]{1,0:T(8,128)(2,1)S(1)}, u32[]{:S(2)}) copy-start(bf16[32,3328]{1,0:T(8,128)(2,1)S(1)} %collective-permute-done.7.refs_9_.refs_6_) | copy-start | bytes 638980
  20.7 18.6 %collective-permute-start.11 = (bf16[32,3328]{1,0:T(8,128)(2,1)S(1)}, bf16[32,3328]{1,0:T(8,128)(2,1)S(1)}, u32[]{:S(2)}, u32[]{:S(2)}) collective-permute-start(bf16[32,3328]{1,0:T(8,128)(2,1)S(1)} %collective-permute-done.10.refs_5_.refs_12_), channel_id=1, source_target_pairs={{0,4},{2,6},{4,0},{6,2},{1,5},{3,7},{5,1},{7,3},{8,12},{10,14},{12... | collective-permute-start | bytes 638984 | tf_op jit(solution)/shard_map/ppermute | solution.py:219
  20.9 22.8 %copy-start.14 = (bf16[32,3328]{1,0:T(8,128)(2,1)}, bf16[32,3328]{1,0:T(8,128)(2,1)S(1)}, u32[]{:S(2)}) copy-start(bf16[32,3328]{1,0:T(8,128)(2,1)S(1)} %collective-permute-done.8.refs_10_.refs_7_) | copy-start | bytes 638980
  20.9 20.3 %collective-permute-start.12 = (bf16[32,3328]{1,0:T(8,128)(2,1)S(1)}, bf16[32,3328]{1,0:T(8,128)(2,1)S(1)}, u32[]{:S(2)}, u32[]{:S(2)}) collective-permute-start(bf16[32,3328]{1,0:T(8,128)(2,1)S(1)} %collective-permute-done.10.refs_5_.refs_12_), channel_id=1, source_target_pairs={{0,2},{2,0},{4,6},{6,4},{1,3},{3,1},{5,7},{7,5},{8,10},{10,8},{12,... | collective-permute-start | bytes 638984 | tf_op jit(solution)/shard_map/ppermute | solution.py:219
  24.6 31.4 %copy-start.6 = (bf16[32,4096]{1,0:T(8,128)(2,1)}, bf16[32,4096]{1,0:T(8,128)(2,1)S(1)}, u32[]{:S(2)}) copy-start(bf16[32,4096]{1,0:T(8,128)(2,1)S(1)} %collective-permute-done.1.refs_2_) | copy-start | bytes 786436
  24.6 16.7 %collective-permute-start.9 = (bf16[32,3328]{1,0:T(8,128)(2,1)S(1)}, bf16[32,3328]{1,0:T(8,128)(2,1)S(1)}, u32[]{:S(2)}, u32[]{:S(2)}) collective-permute-start(bf16[32,3328]{1,0:T(8,128)(2,1)S(1)} %collective-permute-done.7.refs_9_.refs_6_), channel_id=1, source_target_pairs={{0,2},{2,0},{4,6},{6,4},{1,3},{3,1},{5,7},{7,5},{8,10},{10,8},{12,... | collective-permute-start | bytes 638984 | tf_op jit(solution)/shard_map/ppermute | solution.py:219
  24.7 19.0 %copy-start.11 = (bf16[32,4096]{1,0:T(8,128)(2,1)}, bf16[32,4096]{1,0:T(8,128)(2,1)S(1)}, u32[]{:S(2)}) copy-start(bf16[32,4096]{1,0:T(8,128)(2,1)S(1)} %collective-permute-done.3.refs_4_.refs_10_) | copy-start | bytes 786436
  24.7 18.9 %collective-permute-start.4 = (bf16[32,4096]{1,0:T(8,128)(2,1)S(1)}, bf16[32,4096]{1,0:T(8,128)(2,1)S(1)}, u32[]{:S(2)}, u32[]{:S(2)}) collective-permute-start(bf16[32,4096]{1,0:T(8,128)(2,1)S(1)} %collective-permute-done.3.refs_4_.refs_10_), channel_id=1, source_target_pairs={{0,16},{8,24},{16,0},{24,8},{1,17},{9,25},{17,1},{25,9},{2,18},{10... | collective-permute-start | bytes 786440 | tf_op jit(solution)/shard_map/ppermute | solution.py:219
  25.2 30.9 %copy-start.7 = (bf16[32,4096]{1,0:T(8,128)(2,1)}, bf16[32,4096]{1,0:T(8,128)(2,1)S(1)}, u32[]{:S(2)}) copy-start(bf16[32,4096]{1,0:T(8,128)(2,1)S(1)} %collective-permute-done.2.refs_3_) | copy-start | bytes 786436
  25.2 30.9 %collective-permute-start.5 = (bf16[32,4096]{1,0:T(8,128)(2,1)S(1)}, bf16[32,4096]{1,0:T(8,128)(2,1)S(1)}, u32[]{:S(2)}, u32[]{:S(2)}) collective-permute-start(bf16[32,4096]{1,0:T(8,128)(2,1)S(1)} %collective-permute-done.3.refs_4_.refs_10_), channel_id=1, source_target_pairs={{0,8},{8,0},{16,24},{24,16},{1,9},{9,1},{17,25},{25,17},{2,10},{10... | collective-permute-start | bytes 786440 | tf_op jit(solution)/shard_map/ppermute | solution.py:219
  26.3 35.3 %copy-start.1 = (bf16[32,6656]{1,0:T(8,128)(2,1)S(1)}, bf16[32,6656]{1,0:T(8,128)(2,1)}, u32[]{:S(2)}) copy-start(bf16[32,6656]{1,0:T(8,128)(2,1)} %gate_ref.5) | copy-start | bytes 1277956
  26.3 35.3 %copy-start.3 = (bf16[32,6656]{1,0:T(8,128)(2,1)S(1)}, bf16[32,6656]{1,0:T(8,128)(2,1)}, u32[]{:S(2)}) copy-start(bf16[32,6656]{1,0:T(8,128)(2,1)} %up_ref.5) | copy-start | bytes 1277956
  39.3 22.4 %copy-start.9 = (f32[32,3328]{1,0:T(8,128)S(1)}, f32[32,3328]{1,0:T(8,128)}, u32[]{:S(2)}) copy-start(f32[32,3328]{1,0:T(8,128)} %copy-done.8) | copy-start | bytes 1277956
  39.3 18.0 %collective-permute-start.14 = (bf16[32,3328]{1,0:T(8,128)(2,1)S(1)}, bf16[32,3328]{1,0:T(8,128)(2,1)S(1)}, u32[]{:S(2)}, u32[]{:S(2)}) collective-permute-start(bf16[32,3328]{1,0:T(8,128)(2,1)S(1)} %get-tuple-element.23), channel_id=1, source_target_pairs={{0,2},{2,0},{4,6},{6,4},{1,3},{3,1},{5,7},{7,5},{8,10},{10,8},{12,... | collective-permute-start | bytes 638984 | tf_op jit(solution)/shard_map/ppermute | solution.py:219
  41.2 18.2 %collective-permute-start.15 = (bf16[32,3328]{1,0:T(8,128)(2,1)S(1)}, bf16[32,3328]{1,0:T(8,128)(2,1)S(1)}, u32[]{:S(2)}, u32[]{:S(2)}) collective-permute-start(bf16[32,3328]{1,0:T(8,128)(2,1)S(1)} %get-tuple-element.24), channel_id=1, source_target_pairs={{0,4},{2,6},{4,0},{6,2},{1,5},{3,7},{5,1},{7,3},{8,12},{10,14},{12... | collective-permute-start | bytes 638984 | tf_op jit(solution)/shard_map/ppermute | solution.py:219
  41.3 27.7 %copy-start.20 = (bf16[32,3328]{1,0:T(8,128)(2,1)}, bf16[32,3328]{1,0:T(8,128)(2,1)S(1)}, u32[]{:S(2)}) copy-start(bf16[32,3328]{1,0:T(8,128)(2,1)S(1)} %collective-permute-done.9.refs_11_) | copy-start | bytes 638980
  41.3 18.1 %collective-permute-start.16 = (bf16[32,3328]{1,0:T(8,128)(2,1)S(1)}, bf16[32,3328]{1,0:T(8,128)(2,1)S(1)}, u32[]{:S(2)}, u32[]{:S(2)}) collective-permute-start(bf16[32,3328]{1,0:T(8,128)(2,1)S(1)} %get-tuple-element.25), channel_id=1, source_target_pairs={{0,6},{2,4},{4,2},{6,0},{1,7},{3,5},{5,3},{7,1},{8,14},{10,12},{12... | collective-permute-start | bytes 638984 | tf_op jit(solution)/shard_map/ppermute | solution.py:219
  43.7 25.4 %copy-start.17 = (bf16[32,4096]{1,0:T(8,128)(2,1)}, bf16[32,4096]{1,0:T(8,128)(2,1)S(1)}, u32[]{:S(2)}) copy-start(bf16[32,4096]{1,0:T(8,128)(2,1)S(1)} %collective-permute-done.4.refs_5_) | copy-start | bytes 786436
  43.7 25.3 %collective-permute-start.6 = (bf16[32,4096]{1,0:T(8,128)(2,1)S(1)}, bf16[32,4096]{1,0:T(8,128)(2,1)S(1)}, u32[]{:S(2)}, u32[]{:S(2)}) collective-permute-start(bf16[32,4096]{1,0:T(8,128)(2,1)S(1)} %collective-permute-done.4.refs_5_), channel_id=1, source_target_pairs={{0,8},{8,0},{16,24},{24,16},{1,9},{9,1},{17,25},{25,17},{2,10},{10... | collective-permute-start | bytes 786440 | tf_op jit(solution)/shard_map/ppermute | solution.py:219
  56.1 12.9 %collective-permute-start.13 = (bf16[32,3328]{1,0:T(8,128)(2,1)}, bf16[32,3328]{1,0:T(8,128)(2,1)S(1)}, u32[]{:S(2)}, u32[]{:S(2)}) collective-permute-start(bf16[32,3328]{1,0:T(8,128)(2,1)} %copy-done.15), channel_id=1, source_target_pairs={{0,2},{2,0},{4,6},{6,4},{1,3},{3,1},{5,7},{7,5},{8,10},{10,8},{12,... | collective-permute-start | bytes 638984 | tf_op jit(solution)/shard_map/ppermute | solution.py:219
  57.2 24.4 %collective-permute-start.17 = (bf16[32,3328]{1,0:T(8,128)(2,1)S(1)}, bf16[32,3328]{1,0:T(8,128)(2,1)S(1)}, u32[]{:S(2)}, u32[]{:S(2)}) collective-permute-start(bf16[32,3328]{1,0:T(8,128)(2,1)S(1)} %get-tuple-element.29), channel_id=1, source_target_pairs={{0,2},{2,0},{4,6},{6,4},{1,3},{3,1},{5,7},{7,5},{8,10},{10,8},{12,... | collective-permute-start | bytes 638984 | tf_op jit(solution)/shard_map/ppermute | solution.py:219
  59.4 22.2 %collective-permute-start.18 = (bf16[32,3328]{1,0:T(8,128)(2,1)S(1)}, bf16[32,3328]{1,0:T(8,128)(2,1)S(1)}, u32[]{:S(2)}, u32[]{:S(2)}) collective-permute-start(bf16[32,3328]{1,0:T(8,128)(2,1)S(1)} %get-tuple-element.30), channel_id=1, source_target_pairs={{0,4},{2,6},{4,0},{6,2},{1,5},{3,7},{5,1},{7,3},{8,12},{10,14},{12... | collective-permute-start | bytes 638984 | tf_op jit(solution)/shard_map/ppermute | solution.py:219
  59.4 22.3 %collective-permute-start.19 = (bf16[32,3328]{1,0:T(8,128)(2,1)S(1)}, bf16[32,3328]{1,0:T(8,128)(2,1)S(1)}, u32[]{:S(2)}, u32[]{:S(2)}) collective-permute-start(bf16[32,3328]{1,0:T(8,128)(2,1)S(1)} %get-tuple-element.31), channel_id=1, source_target_pairs={{0,6},{2,4},{4,2},{6,0},{1,7},{3,5},{5,3},{7,1},{8,14},{10,12},{12... | collective-permute-start | bytes 638984 | tf_op jit(solution)/shard_map/ppermute | solution.py:219
  (10 other events, 37.7 us)
